TPU v7x, 32 devices: a whole 2x2x4 slice. The times are simulated.
32 devices in a mesh: row: 8 (over z, x), col: 4 (over y, core).
Axes of the slice: x: 2, y: 2, z: 4, core: 2. Of those that a mesh axis runs over, the one named last changes fastest.
Arguments:
- homolog_tensor: bfloat16 [256, 128, 256], P('row', 'col'), may hold values from -6 to 6
- pairwise_tensor: bfloat16 [128, 128, 128], P('row', 'col'), may hold values from -6 to 6
- genuine_amino_flags: int32 [128], replicated, may hold values 0 or 1
- polymer_identity: int32 [128], replicated, may hold values from 0 to 3, never falling along the last dimension, each value on 1 to 64 neighbouring positions
- asking_weights: bfloat16 [256, 256], replicated, may hold values from -0.375 to 0.375
- attend_sigmoid_weights: bfloat16 [256, 256], replicated, may hold values from -0.375 to 0.375
- lookup_content_weights: bfloat16 [256, 512], replicated, may hold values from -0.375 to 0.375
- attend_final_weights: bfloat16 [256, 256], replicated, may hold values from -0.375 to 0.375
- pairwise_logit_weights: bfloat16 [128, 8], replicated, may hold values from -20 to 20
- crosspolymer_offset: float32 [8], replicated, may hold values from -2 to 2
- outgoing_link_weights: bfloat16 [128, 256], replicated, may hold values from -0.5 to 0.5
- incoming_link_weights: bfloat16 [128, 256], replicated, may hold values from -0.5 to 0.5
- trimult_sigmoid_weights: bfloat16 [128, 128], replicated, may hold values from -0.5 to 0.5
- trimult_final_weights: bfloat16 [128, 128], replicated, may hold values from -0.5 to 0.5
Outputs:
- attended_homologs: bfloat16 [256, 128, 256], P('row', 'col')
- pair_output: bfloat16 [128, 128, 128], P('row', 'col')
Inputs may be any that keep to these rules, and one draw needn't show every extreme that they name: `polymer_identity`: chain ids never fall along the residues; each chain has 1 to 64 residues and one has exactly that many.
All inputs are finite; a program needn't handle non-finite values.
Results may differ from a plain program's by a relative error of at most 0.0035.
The roundings to bfloat16 on the way count: a program that leaves them out, or rounds other values in their place, can miss the bound.
Values may be sent and summed in bfloat16 or wider, within the bound.
A program may use at most 64 MiB of HBM per device.

v0:
```python
import jax
import jax.numpy as jnp
from jax import lax
from jax.sharding import PartitionSpec as P


def from_root(array, axis, root):
    mine = lax.axis_index(axis) == root
    return lax.psum(jnp.where(mine, array, jnp.zeros_like(array)), axis)


def standardize_features(tensor):
    tensor = tensor.astype(jnp.float32)
    center = tensor - jnp.mean(tensor, axis=-1, keepdims=True)
    spread = jnp.mean(center * center, axis=-1, keepdims=True)
    return center * lax.rsqrt(spread + 1e-05)


def edges(pair_norm, weight, mask_rows, width):
    projected = jnp.dot(pair_norm, weight, preferred_element_type=jnp.float32)
    edge_vals = (
        mask_rows * jax.nn.sigmoid(projected[..., :width]) * projected[..., width:]
    ).astype(jnp.bfloat16)
    return jnp.transpose(edge_vals, (2, 0, 1))


def local(
    homolog_tensor,
    pairwise_tensor,
    genuine_amino_flags,
    polymer_identity,
    asking_weights,
    attend_sigmoid_weights,
    lookup_content_weights,
    attend_final_weights,
    pairwise_logit_weights,
    crosspolymer_offset,
    outgoing_link_weights,
    incoming_link_weights,
    trimult_sigmoid_weights,
    trimult_final_weights,
):
    row_count = lax.axis_size("row")
    col_count = lax.axis_size("col")
    row_index = lax.axis_index("row")
    col_index = lax.axis_index("col")
    homolog_entries, amino_positions, feature_depth = homolog_tensor.shape
    res_rows = pairwise_tensor.shape[0]
    pair_width = pairwise_tensor.shape[2]
    row_ratio = row_count // col_count
    head_count = pairwise_logit_weights.shape[1]
    inner_width = asking_weights.shape[1]
    per_head_width = inner_width // head_count
    standardized_homologs = standardize_features(homolog_tensor).astype(jnp.bfloat16)
    pair_norm = standardize_features(pairwise_tensor).astype(jnp.bfloat16)
    local_bias = jnp.einsum(
        "ijc,ch->hij", pair_norm, pairwise_logit_weights, preferred_element_type=jnp.float32
    ).astype(jnp.bfloat16)
    row_bias = lax.all_gather(local_bias, "col", axis=2, tiled=True)
    queries = (
        jnp.dot(standardized_homologs, asking_weights, preferred_element_type=jnp.float32)
        * per_head_width ** (-0.5)
    ).astype(jnp.bfloat16)
    queries = queries.reshape(homolog_entries, amino_positions, head_count, per_head_width)
    gate_activation = jax.nn.sigmoid(
        jnp.dot(standardized_homologs, attend_sigmoid_weights, preferred_element_type=jnp.float32)
    )
    all_bias = lax.all_gather(row_bias, "row", axis=1, tiled=True)
    bias_block = lax.dynamic_slice_in_dim(all_bias, col_index * amino_positions, amino_positions, 1)
    query_chain = lax.dynamic_slice_in_dim(
        polymer_identity, col_index * amino_positions, amino_positions, 0
    )
    cross_chain = (query_chain[:, None] != polymer_identity[None, :]).astype(jnp.float32)
    extra_bias = (
        bias_block.astype(jnp.float32) + crosspolymer_offset[:, None, None] * cross_chain[None]
    )
    keep_all = genuine_amino_flags > 0
    key_value = jnp.dot(
        lax.all_gather(standardized_homologs, "col", axis=1, tiled=True),
        lookup_content_weights,
        preferred_element_type=jnp.float32,
    ).astype(jnp.bfloat16)
    piece_len = key_value.shape[1]
    key_rows = key_value[..., :inner_width].reshape(
        homolog_entries, piece_len, head_count, per_head_width
    )
    value_rows = key_value[..., inner_width:].reshape(
        homolog_entries, piece_len, head_count, per_head_width
    )
    scores = jnp.einsum("sqhd,skhd->shqk", queries, key_rows, preferred_element_type=jnp.float32)
    scores = scores + extra_bias[None]
    scores = jnp.where(keep_all, scores, -1000000000.0)
    peak_old = jnp.full((homolog_entries, head_count, amino_positions), -jnp.inf, jnp.float32)
    total_old = jnp.zeros((homolog_entries, head_count, amino_positions), jnp.float32)
    accum_old = jnp.zeros(
        (homolog_entries, head_count, amino_positions, per_head_width), jnp.float32
    )
    peak_now = jnp.max(scores, axis=-1)
    factor = jnp.exp(peak_old - peak_now)
    exp_scores = jnp.exp(scores - peak_now[..., None])
    total_now = total_old * factor + jnp.sum(exp_scores, axis=-1)
    accum_now = accum_old * factor[..., None] + jnp.einsum(
        "shqk,skhd->shqd",
        exp_scores.astype(jnp.bfloat16),
        value_rows,
        preferred_element_type=jnp.float32,
    )
    peak_now, total_now, accum_now = (peak_now, total_now, accum_now)
    attended = accum_now / total_now[..., None]
    attended = jnp.transpose(attended, (0, 2, 1, 3)).reshape(
        homolog_entries, amino_positions, inner_width
    )
    gated_output = (gate_activation * attended).astype(jnp.bfloat16)
    attended_homologs = (
        homolog_tensor.astype(jnp.float32)
        + jnp.dot(gated_output, attend_final_weights, preferred_element_type=jnp.float32)
    ).astype(jnp.bfloat16)
    mask_rows = lax.dynamic_slice_in_dim(
        genuine_amino_flags, row_index * res_rows, res_rows, 0
    ).astype(jnp.float32)[:, None, None]
    left_tri = edges(pair_norm, outgoing_link_weights, mask_rows, pair_width)
    right_tri = edges(pair_norm, incoming_link_weights, mask_rows, pair_width)
    left_cols = lax.all_gather(left_tri, "row", axis=1, tiled=True)
    left_part = lax.dynamic_slice_in_dim(left_cols, row_index % row_ratio * res_rows, res_rows, 2)
    left_mine = from_root(left_part, "col", row_index // row_ratio)
    product = jnp.einsum(
        "cki,ckj->cij",
        left_mine,
        lax.all_gather(right_tri, "row", axis=1, tiled=True),
        preferred_element_type=jnp.float32,
    )
    product_norm = standardize_features(jnp.transpose(product, (1, 2, 0))).astype(jnp.bfloat16)
    tri_gate = jax.nn.sigmoid(
        jnp.dot(pair_norm, trimult_sigmoid_weights, preferred_element_type=jnp.float32)
    )
    update = jnp.dot(product_norm, trimult_final_weights, preferred_element_type=jnp.float32)
    pair_output = (pairwise_tensor.astype(jnp.float32) + tri_gate * update).astype(jnp.bfloat16)
    return (attended_homologs, pair_output)


def solution(mesh):
    in_specs = (
        P("row", "col", None),
        P("row", "col", None),
        P(),
        P(),
        P(),
        P(),
        P(),
        P(),
        P(),
        P(),
        P(),
        P(),
        P(),
        P(),
    )
    out_specs = (P("row", "col", None), P("row", "col", None))
    return jax.shard_map(local, mesh=mesh, in_specs=in_specs, out_specs=out_specs, check_vma=False)
```

profile of v0, /device:TPU:0, one launch (start us, length us, event | category | flops | bytes accessed | tf_op | source)
XLA Modules:
  0.0 198.1 jit_solution(17099859120784856583)
XLA Ops:
  7.2 0.0 all-gather.6.cloned.1.call-start
  7.2 1.1 convert_reduce_fusion.1
  8.4 1.2 fusion.32
  9.6 1.2 fusion.51
  10.8 1.2 fusion.53
  12.1 0.8 dynamic-slice_convert_fusion
  12.8 0.9 fusion.50
  13.7 0.0 all-gather.8.cloned.1.call-start
  13.8 0.7 all-gather.8.cloned.1.call-update
  14.5 0.0 all-reduce.2.cloned.1.call-start
  14.6 1.3 convert_reduce_fusion
  15.8 0.4 fusion.26
  16.2 40.5 %all-gather.6.cloned.1.call-done = bf16[128,128,32]{0,2,1:T(8,128)(2,1)} async-done(((bf16[128,16,32]{0,2,1:T(8,128)(2,1)}), bf16[128,128,32]{0,2,1:T(8,128)(2,1)}) %all-gather.6.cloned.1.call-update) | async-done | bytes 1048592 | tf_op jit(solution)/shard_map/all_gather | solution.py:123
  56.7 1.1 constant_dynamic-slice_fusion
  57.8 0.7 copy.41
  58.6 0.9 broadcast_select_fusion
  59.4 0.0 all-reduce.2.cloned.1.call-update
  59.5 0.0 all-gather.4.cloned.1.call-start
  59.5 1.1 fusion.27
  60.7 0.3 fusion.25
  61.1 0.1 copy.33
  61.2 5.8 %all_gather.16 = bf16[8,16,128]{1,0,2:T(8,128)(2,1)S(1)} all-gather(bf16[8,16,32]{1,0,2:T(8,128)(2,1)S(1)} %copy.33), channel_id=1, replica_groups=mesh['row'=8,'col'=4] {'col'}, dimensions={2}, use_global_device_ids=true | all-gather | bytes 40960 | tf_op jit(solution)/shard_map/all_gather | solution.py:59
  67.0 0.2 copy.34
  67.2 0.1 dynamic_slice.13
  67.3 31.4 %all_gather.17 = bf16[8,128,128]{2,0,1:T(8,128)(2,1)S(1)} all-gather(bf16[8,16,128]{2,0,1:T(8,128)(2,1)S(1)} %copy.34), channel_id=1, replica_groups=mesh['row'=8,'col'=4] {'row'}, dimensions={1}, use_global_device_ids=true | all-gather | bytes 294912 | tf_op jit(solution)/shard_map/all_gather | solution.py:68
  98.7 0.1 compare_convert_fusion
  98.8 0.1 multiply_add_fusion
  98.9 1.3 fusion.17
  100.2 2.6 %reshape.94 = bf16[32,32,8,32]{3,2,1,0:T(8,128)(2,1)S(1)} reshape(bf16[32,32,256]{2,1,0:T(8,128)(2,1)} %fusion.17) | data formatting | bytes 1048576 | tf_op jit(solution)/shard_map/reshape | solution.py:64
  102.9 0.3 fusion.23
  103.2 0.0 all-gather.8.cloned.1.call-done
  103.2 7.3 %copy.39 = bf16[128,128,32]{2,1,0:T(8,128)(2,1)} copy(bf16[128,128,32]{0,2,1:T(8,128)(2,1)} %all-gather.8.cloned.1.call-done) | data formatting | bytes 2097152 | tf_op jit(solution)/shard_map/all_gather | solution.py:129
  110.5 23.2 %all-reduce.2.cloned.1.call-done = bf16[128,128,16]{1,2,0:T(8,128)(2,1)} async-done(((bf16[128,128,16]{1,2,0:T(8,128)(2,1)}), bf16[128,128,16]{1,2,0:T(8,128)(2,1)}) %all-reduce.2.cloned.1.call-update) | async-done | bytes 524304 | tf_op jit(solution)/shard_map/psum | solution.py:9
  133.7 3.6 %fusion.68 = (f32[16,32]{1,0:T(8,128)S(1)}, f32[16,32,128]{1,0,2:T(8,128)S(1)}) fusion(bf16[128,128,16]{1,2,0:T(8,128)(2,1)} %all-reduce.2.cloned.1.call-done, bf16[128,128,32]{2,1,0:T(8,128)(2,1)} %copy.39), kind=kOutput, calls=%fused_computation.94 | convolution fusion | flops 16842240 | bytes 1837056 | tf_op jit(solution)/shard_map/cki,ckj->cij/dot_general | solution.py:126
  137.3 0.2 multiply_reduce_fusion
  137.5 0.1 multiply_convert_fusion
  137.6 1.0 fusion.24
  138.6 19.7 %all-gather.4.cloned.1.call-done = bf16[32,128,256]{2,1,0:T(8,128)(2,1)} async-done(((bf16[32,32,256]{2,1,0:T(8,128)(2,1)}), bf16[32,128,256]{2,1,0:T(8,128)(2,1)}) %all-gather.4.cloned.1.call-update) | async-done | bytes 2097168 | tf_op jit(solution)/shard_map/all_gather | solution.py:79
  158.3 2.8 %convolution_convert_fusion = bf16[32,128,512]{2,1,0:T(8,128)(2,1)S(1)} fusion(bf16[32,128,256]{2,1,0:T(8,128)(2,1)} %all-gather.4.cloned.1.call-done, bf16[256,512]{1,0:T(8,128)(2,1)S(1)} %copy-done), kind=kOutput, calls=%fused_computation.7 | convolution fusion | flops 1075838976 | bytes 6553600 | tf_op jit(solution)/shard_map/dot_general | solution.py:78
  161.2 2.6 %fusion.67 = (bf16[32,128,256]{2,1,0:T(8,128)(2,1)}, bf16[32,128,256]{2,1,0:T(8,128)(2,1)}) fusion(bf16[32,128,512]{2,1,0:T(8,128)(2,1)S(1)} %convolution_convert_fusion), kind=kLoop, calls=%fused_computation.93 | loop fusion | bytes 8388608 | tf_op jit(solution)/shard_map/slice | solution.py:84
  163.8 4.1 %copy.36 = bf16[32,128,256]{1,2,0:T(8,128)(2,1)} copy(bf16[32,128,256]{2,1,0:T(8,128)(2,1)} %get-tuple-element.3) | data formatting | bytes 4194304 | tf_op jit(solution)/shard_map/slice | solution.py:87
  167.8 4.1 %copy.31 = bf16[32,128,256]{1,2,0:T(8,128)(2,1)} copy(bf16[32,128,256]{2,1,0:T(8,128)(2,1)} %get-tuple-element.2) | data formatting | bytes 4194304 | tf_op jit(solution)/shard_map/slice | solution.py:84
  171.9 3.0 %fusion.1 = (f32[32,8,32]{2,1,0:T(8,128)S(1)}, f32[32,8,32,128]{3,2,1,0:T(8,128)S(1)}) fusion(f32[8,32,128]{2,1,0:T(8,128)S(1)} %copy.35, pred[128]{0:T(512)(128)(4,1)S(1)} %broadcast_compare_fusion, bf16[32,128,8,32]{1,3,2,0:T(8,128)(2,1)} %bitcast.55, bf16[32,32,8,32]{3,2,1,0:T(8,128)(2,1)S(1)} %reshape.94), kind=kOutput, calls=%fused_computation.4 | convolution fusion | flops 70246400 | bytes 6979712 | tf_op jit(solution)/shard_map/sqhd,skhd->shqk/dot_general | solution.py:90
  174.9 2.7 %fusion.2 = f32[32,8,32]{2,1,0:T(8,128)S(1)} fusion(f32[32,8,32,128]{3,2,1,0:T(8,128)S(1)} %get-tuple-element.7, f32[32,8,32]{2,1,0:T(8,128)S(1)} %get-tuple-element.6, f32[8,32,128]{2,1,0:T(8,128)S(1)} %copy.35, pred[128]{0:T(512)(128)(4,1)S(1)} %broadcast_compare_fusion), kind=kLoop, calls=%fused_computation.5 | loop fusion | flops 4186112 | bytes 4391040 | tf_op jit(solution)/shard_map/reduce_sum | solution.py:101
  177.6 3.3 %fusion = f32[32,32,8,32]{3,1,2,0:T(8,128)S(1)} fusion(bf16[32,128,8,32]{1,3,2,0:T(8,128)(2,1)S(1)} %bitcast.56, f32[32,8,32,128]{3,2,1,0:T(8,128)S(1)} %get-tuple-element.7, f32[32,32,8]{1,2,0:T(8,128)S(1)} %bitcast_add_fusion.1, f32[32,8,32]{2,1,0:T(8,128)S(1)} %get-tuple-element.6, f32[32,32,8]{1,2,0:T(8,128)S(1)} %multiply_bitcast_fusion, ...), kind=kOutput, calls=%fused_computation.1 | convolution fusion | flops 71827456 | bytes 7569536 | tf_op jit(solution)/shard_map/shqk,skhd->shqd/dot_general | solution.py:102
  181.0 5.7 %copy.37 = f32[32,32,8,32]{3,2,1,0:T(8,128)} copy(f32[32,32,8,32]{3,1,2,0:T(8,128)S(1)} %fusion) | data formatting | bytes 2097152 | tf_op jit(solution)/shard_map/div | solution.py:109
  186.7 3.4 %reshape.97 = f32[32,32,256]{2,1,0:T(8,128)S(1)} reshape(f32[32,32,8,32]{3,2,1,0:T(8,128)} %copy.37) | data formatting | bytes 2097152 | tf_op jit(solution)/shard_map/reshape | solution.py:110
  190.1 1.4 fusion.16
  (38 shorter events, 0.2 us)
Async XLA Ops:
  7.2 151.2 %copy-start = (bf16[256,512]{1,0:T(8,128)(2,1)S(1)}, bf16[256,512]{1,0:T(8,128)(2,1)}, u32[]{:S(2)}) copy-start(bf16[256,512]{1,0:T(8,128)(2,1)} %param.20) | copy-start | bytes 786436
  7.2 8.7 %copy-start.1 = (bf16[32,32,256]{2,1,0:T(8,128)(2,1)S(1)}, bf16[32,32,256]{2,1,0:T(8,128)(2,1)}, u32[]{:S(2)}) copy-start(bf16[32,32,256]{2,1,0:T(8,128)(2,1)} %param.14) | copy-start | bytes 1572868
  7.2 49.6 %all-gather.6.cloned.1.call-start = ((), (), s32[]{:S(2)}) async-start(), calls=%async_computation.1 | async-start | bytes 1179648 | tf_op jit(solution)/shard_map/all_gather | solution.py:123
  12.0 48.7 %copy-start.2 = (bf16[16,32,128]{2,1,0:T(8,128)(2,1)S(1)}, bf16[16,32,128]{2,1,0:T(8,128)(2,1)}, u32[]{:S(2)}) copy-start(bf16[16,32,128]{2,1,0:T(8,128)(2,1)} %param.15) | copy-start | bytes 393220
  12.0 48.7 %copy-start.11 = (bf16[128,8]{0,1:T(8,128)(2,1)S(1)}, bf16[128,8]{0,1:T(8,128)(2,1)}, u32[]{:S(2)}) copy-start(bf16[128,8]{0,1:T(8,128)(2,1)} %param.22) | copy-start | bytes 6148
  13.7 53.5 %copy-start.6 = (s32[128]{0:T(128)S(1)}, s32[128]{0:T(128)}, u32[]{:S(2)}) copy-start(s32[128]{0:T(128)} %param.17) | copy-start | bytes 1540
  13.7 85.1 %copy-start.5 = (f32[8]{0:T(128)S(1)}, f32[8]{0:T(128)}, u32[]{:S(2)}) copy-start(f32[8]{0:T(128)} %param.23) | copy-start | bytes 100
  13.7 89.5 %all-gather.8.cloned.1.call-start = ((), (), s32[]{:S(2)}) async-start(), calls=%async_computation.3 | async-start | bytes 1179648 | tf_op jit(solution)/shard_map/all_gather | solution.py:129
  13.8 85.1 %copy-start.7 = (bf16[256,256]{1,0:T(8,128)(2,1)S(1)}, bf16[256,256]{1,0:T(8,128)(2,1)}, u32[]{:S(2)}) copy-start(bf16[256,256]{1,0:T(8,128)(2,1)} %param.18) | copy-start | bytes 393220
  14.5 119.2 %all-reduce.2.cloned.1.call-start = ((), (), s32[]{:S(2)}) async-start(), calls=%async_computation.2 | async-start | bytes 1048576 | tf_op jit(solution)/shard_map/psum | solution.py:9
  59.4 43.4 %copy-start.12 = (s32[128]{0:T(128)S(1)}, s32[128]{0:T(128)}, u32[]{:S(2)}) copy-start(s32[128]{0:T(128)} %param.16) | copy-start | bytes 1540
  59.4 43.4 %copy-start.10 = (bf16[128,128]{1,0:T(8,128)(2,1)S(1)}, bf16[128,128]{1,0:T(8,128)(2,1)}, u32[]{:S(2)}) copy-start(bf16[128,128]{1,0:T(8,128)(2,1)} %param.26) | copy-start | bytes 98308
  59.5 98.9 %all-gather.4.cloned.1.call-start = ((), (), s32[]{:S(2)}) async-start(), calls=%async_computation | async-start | bytes 2621440 | tf_op jit(solution)/shard_map/all_gather | solution.py:79
  110.5 27.1 %copy-start.4 = (bf16[128,128]{1,0:T(8,128)(2,1)S(1)}, bf16[128,128]{1,0:T(8,128)(2,1)}, u32[]{:S(2)}) copy-start(bf16[128,128]{1,0:T(8,128)(2,1)} %param.27) | copy-start | bytes 98308
  174.9 2.8 %copy-start.3 = (bf16[32,128,256]{1,2,0:T(8,128)(2,1)S(1)}, bf16[32,128,256]{1,2,0:T(8,128)(2,1)}, u32[]{:S(2)}) copy-start(bf16[32,128,256]{1,2,0:T(8,128)(2,1)} %copy.36) | copy-start | bytes 6291460
  186.7 3.4 %copy-start.8 = (bf16[256,256]{1,0:T(8,128)(2,1)S(1)}, bf16[256,256]{1,0:T(8,128)(2,1)}, u32[]{:S(2)}) copy-start(bf16[256,256]{1,0:T(8,128)(2,1)} %param.21) | copy-start | bytes 393220
  186.7 3.4 %copy-start.9 = (bf16[256,256]{1,0:T(8,128)(2,1)S(1)}, bf16[256,256]{1,0:T(8,128)(2,1)}, u32[]{:S(2)}) copy-start(bf16[256,256]{1,0:T(8,128)(2,1)} %param.19) | copy-start | bytes 393220
Sparse Core Ops, SparseCore 0:
  13.9 42.8 all-gather.5
  59.4 39.8 all-gather.7
  101.7 31.9 all-reduce.1
  135.7 22.5 all-gather.3
where the time goes:
time: 199 us; the launch traced here: 198 us
  waiting for transfers between devices  84.2 us (42%)
  blocking collectives  37.2 us (19%)
  local copies, waits for them, and re-layouts  32.1 us (16%)
  matrix products  19.5 us (10%)
  between operations  14.1 us (7%)
  other arithmetic  10.8 us (5%)
    all_gather x1, waiting for transfers between devices, local(): left_cols = lax.all_gather(left_tri, 'row', axis=1, tiled=True)  40.5 us
    all_gather x1, blocking collectives, local(): all_bias = lax.all_gather(row_bias, 'row', axis=1, tiled=True)  31.4 us
    psum x1, waiting for transfers between devices, from_root(): return lax.psum(jnp.where(mine, array, jnp.zeros_like(array)), axis)  23.2 us
    all_gather x1, waiting for transfers between devices, local(): lax.all_gather(standardized_homologs, 'col', axis=1, tiled=True)  19.7 us
    all_gather x1, local copies, waits for them, and re-layouts, local(): lax.all_gather(right_tri, 'row', axis=1, tiled=True)  7.27 us
    slice x2, local copies, waits for them, and re-layouts, local(): key_value[..., :inner_width]  6.66 us
    all_gather x1, blocking collectives, local(): row_bias = lax.all_gather(local_bias, 'col', axis=2, tiled=True)  5.79 us
    div x1, local copies, waits for them, and re-layouts, local(): attended = accum_now / total_now[..., None]  5.73 us
  transfers between devices with their start and end apart: 4, of which 3 were waited for; matrix products, arithmetic and copies ran while one was open for 11% of the time, Pallas kernels for 0%

commit v1 on v0

--- a/solution.py
+++ b/solution.py
@@ -1,7 +1,381 @@
+import functools
+
 import jax
 import jax.numpy as jnp
 from jax import lax
+from jax.experimental import pallas as pl
+from jax.experimental.pallas import tpu as pltpu
 from jax.sharding import PartitionSpec as P
+
+MESH = pl.DeviceIdType.MESH
+F32 = jnp.float32
+BF16 = jnp.bfloat16
+
+
+def dot(a, b, contract=((1,), (0,))):
+    return lax.dot_general(a, b, (contract, ((), ())), preferred_element_type=F32)
+
+
+def normalize(x, axis):
+    center = x - jnp.mean(x, axis=axis, keepdims=True)
+    spread = jnp.mean(center * center, axis=axis, keepdims=True)
+    return center * lax.rsqrt(spread + 1e-05)
+
+
+def lane_blocks(shape, width):
+    return lax.broadcasted_iota(jnp.int32, shape, len(shape) - 1) // width
+
+
+def shift_lanes(x, amount):
+    amount = amount % x.shape[-1]
+    return x if amount == 0 else pltpu.roll(x, amount, x.ndim - 1)
+
+
+def fused(
+    dims,
+    x_ref,
+    pair_ref,
+    mask_ref,
+    keep_ref,
+    cross_ref,
+    offset_ref,
+    wq_ref,
+    wg_ref,
+    wkv_ref,
+    wo_ref,
+    edge_w_ref,
+    tri_gate_w_ref,
+    tri_out_w_ref,
+    msa_out_ref,
+    pair_out_ref,
+    hx,
+    hout,
+    send,
+    recv,
+    psend,
+    precv,
+    zed,
+    zprod,
+    extra,
+    pn_ref,
+    x_send_sem,
+    x_recv_sem,
+    e_send_sem,
+    e_recv_sem,
+    p_send_sem,
+    p_recv_sem,
+    o_send_sem,
+    o_recv_sem,
+):
+    rows, cols, heads, channels = dims
+    count = rows * cols
+    row = lax.axis_index("row")
+    col = lax.axis_index("col")
+    me = row * cols + col
+    seqs, residues, depth = hx.shape[1:]
+    total_res = cols * residues
+    width = depth // heads
+    pair_rows, pair_cols, cz = pair_ref.shape
+    positions = pair_rows * pair_cols
+
+    def other(step):
+        peer = lax.rem(me + step, count)
+        return peer // cols, lax.rem(peer, cols)
+
+    barrier = pltpu.get_barrier_semaphore()
+
+    def greet(step, carry):
+        pl.semaphore_signal(barrier, inc=1, device_id=other(step), device_id_type=MESH)
+        return carry
+
+    lax.fori_loop(1, count, greet, 0)
+    pl.semaphore_wait(barrier, count - 1)
+
+    for step in range(1, cols):
+        peer = lax.rem(col + step, cols)
+        pltpu.make_async_remote_copy(
+            src_ref=x_ref.at[pl.ds(peer * seqs, seqs)],
+            dst_ref=hx.at[col],
+            send_sem=x_send_sem,
+            recv_sem=x_recv_sem,
+            device_id=(row, peer),
+            device_id_type=MESH,
+        ).start()
+    hx[pl.ds(col, 1)] = x_ref[pl.ds(col * seqs, seqs)][None]
+
+    with jax.named_scope("pair_edges_and_bias"):
+        pair = pair_ref[...].astype(F32).reshape(positions, cz)
+        pn = normalize(pair, -1).astype(BF16)
+        pn_ref[...] = pn
+        proj = dot(edge_w_ref[...], pn, ((1,), (1,)))
+        both = 2 * cz
+        edge = mask_ref[...] * jax.nn.sigmoid(proj[:both]) * proj[both : 2 * both]
+        half = positions // 2
+        edge = edge.reshape(count, 8, positions)
+        bias = proj[2 * both : 2 * both + 8]
+        send[:, :16, :] = jnp.concatenate(
+            [edge[:, :, :half], edge[:, :, half:]], axis=1
+        ).astype(BF16)
+        bias = jnp.concatenate([bias[:, :half], bias[:, half:]], axis=0).astype(BF16)
+        send[:, 16:, :] = jnp.broadcast_to(bias[None], (count, 16, half))
+
+    def push(step, carry):
+        to_row, to_col = other(step)
+        slot = to_row * cols + to_col
+        pltpu.make_async_remote_copy(
+            src_ref=send.at[slot],
+            dst_ref=recv.at[me],
+            send_sem=e_send_sem,
+            recv_sem=e_recv_sem,
+            device_id=(to_row, to_col),
+            device_id_type=MESH,
+        ).start()
+        return carry
+
+    lax.fori_loop(1, count, push, 0)
+    recv[pl.ds(me, 1)] = send[pl.ds(me, 1)]
+
+    def wait_all(ref, sem):
+        part = ref.at[pl.ds(0, count - 1)]
+        pltpu.make_async_copy(part, part, sem).wait()
+
+    wait_all(recv, e_recv_sem)
+
+    block = pair_cols
+    lanes = total_res
+    per_tile = lanes // block
+    where_block = lane_blocks((16 * rows, lanes), block)
+    with jax.named_scope("to_matrices"):
+        for part in range(2):
+            for tile in range(half // lanes):
+                taken = recv[:, part * 16 : part * 16 + 16, tile * lanes : (tile + 1) * lanes]
+                taken = taken.astype(F32).reshape(rows, cols, 16, lanes)
+                pieces = [taken[:, c].reshape(16 * rows, lanes) for c in range(cols)]
+                for k in range(per_tile):
+                    merged = shift_lanes(pieces[0], (0 - k) * block)
+                    for c in range(1, cols):
+                        merged = jnp.where(
+                            where_block == c, shift_lanes(pieces[c], (c - k) * block), merged
+                        )
+                    zed[part, pl.ds(tile * per_tile + k, 16 * rows, stride=8), :] = merged
+
+    def matrix(part, q):
+        return zed[part].reshape(2 * rows, 8, 8, lanes)[:, q].reshape(total_res, lanes)
+
+    with jax.named_scope("triangle_product"):
+        mine = channels // count
+        for ch in range(mine):
+            left = matrix(0, ch).T.astype(BF16)
+            right = matrix(0, mine + ch).astype(BF16)
+            product = dot(left, right).reshape(2 * rows, 8, lanes)
+            zprod[:, ch] = product
+        where_small = lane_blocks((2 * rows * mine, lanes), block)
+        for tile in range(half // lanes):
+            taken = [
+                zprod.reshape(2 * rows * mine * 8, lanes)[
+                    pl.ds(tile * per_tile + k, 2 * rows * mine, stride=8), :
+                ]
+                for k in range(per_tile)
+            ]
+            merged_all = []
+            for c in range(cols):
+                merged = shift_lanes(taken[0], (0 - c) * block)
+                for k in range(1, per_tile):
+                    merged = jnp.where(
+                        where_small == k, shift_lanes(taken[k], (k - c) * block), merged
+                    )
+                merged_all.append(merged.reshape(rows, 2 * mine, lanes))
+            psend[:, :, tile * lanes : (tile + 1) * lanes] = jnp.stack(
+                merged_all, axis=1
+            ).reshape(count, 2 * mine, lanes)
+
+    def push_product(step, carry):
+        to_row, to_col = other(step)
+        slot = to_row * cols + to_col
+        pltpu.make_async_remote_copy(
+            src_ref=psend.at[slot],
+            dst_ref=precv.at[me],
+            send_sem=p_send_sem,
+            recv_sem=p_recv_sem,
+            device_id=(to_row, to_col),
+            device_id_type=MESH,
+        ).start()
+        return carry
+
+    lax.fori_loop(1, count, push_product, 0)
+    precv[pl.ds(me, 1)] = psend[pl.ds(me, 1)]
+
+    with jax.named_scope("attention_bias"):
+        for h in range(heads):
+            extra[h] = matrix(1, h) + offset_ref[h] * cross_ref[...]
+
+    three = hx.at[pl.ds(0, cols - 1)]
+    pltpu.make_async_copy(three, three, x_recv_sem).wait()
+
+    keep = keep_ref[...] > 0
+    head_of = lane_blocks((total_res, depth), width)
+
+    def attend(s, carry):
+        x = hx[:, s].reshape(total_res, depth).astype(F32)
+        xn = normalize(x, -1).astype(BF16)
+        queries = (dot(xn, wq_ref[...]) * width ** (-0.5)).astype(BF16)
+        kv = dot(xn, wkv_ref[...])
+        keys, values = kv[:, :depth], kv[:, depth:]
+        gate = jax.nn.sigmoid(dot(xn, wg_ref[...]))
+        key_stack = jnp.concatenate(
+            [jnp.where(head_of == h, keys, 0.0).astype(BF16) for h in range(heads)], axis=0
+        )
+        value_stack = jnp.concatenate(
+            [jnp.where(head_of == h, values, 0.0).astype(BF16) for h in range(heads)], axis=0
+        )
+        scores = dot(queries, key_stack, ((1,), (1,)))
+        probs = []
+        total = jnp.ones((total_res, depth), F32)
+        for h in range(heads):
+            one = scores[:, h * total_res : (h + 1) * total_res] + extra[h]
+            one = jnp.where(keep, one, -1000000000.0)
+            one = jnp.exp(one - jnp.max(one, axis=-1, keepdims=True))
+            total = jnp.where(head_of == h, jnp.sum(one, axis=-1, keepdims=True), total)
+            probs.append(one.astype(BF16))
+        attended = dot(jnp.concatenate(probs, axis=1), value_stack) / total
+        gated = (gate * attended).astype(BF16)
+        result = (x + dot(gated, wo_ref[...])).astype(BF16)
+        hout[:, s] = result.reshape(cols, residues, depth)
+        for step in range(1, cols):
+            peer = lax.rem(col + step, cols)
+            pltpu.make_async_remote_copy(
+                src_ref=hout.at[peer, s],
+                dst_ref=msa_out_ref.at[col * seqs + s],
+                send_sem=o_send_sem,
+                recv_sem=o_recv_sem,
+                device_id=(row, peer),
+                device_id_type=MESH,
+            ).start()
+        msa_out_ref[pl.ds(col * seqs + s, 1)] = hout[pl.ds(col, 1), s]
+        return carry
+
+    with jax.named_scope("row_attention"):
+        lax.fori_loop(0, seqs, attend, 0)
+
+    wait_all(precv, p_recv_sem)
+    with jax.named_scope("pair_update"):
+        product = precv[...]
+        in_half = lax.broadcasted_iota(jnp.int32, (8, half), 0) < mine
+
+        def spread_halves(partial):
+            low = jnp.sum(jnp.where(in_half, partial, 0.0), axis=0, keepdims=True)
+            high = jnp.sum(jnp.where(in_half, 0.0, partial), axis=0, keepdims=True)
+            return jnp.where(in_half, low, high) / channels
+
+        center = product - spread_halves(jnp.sum(product, axis=0))[None]
+        spread = spread_halves(jnp.sum(center * center, axis=0))
+        norm = (center * lax.rsqrt(spread + 1e-05)[None]).reshape(count * 8, half)
+        update = dot(norm.T.astype(BF16), tri_out_w_ref[...])
+        update = jnp.concatenate([update[:, :cz], update[:, cz:]], axis=0)
+        tri_gate = jax.nn.sigmoid(dot(pn_ref[...], tri_gate_w_ref[...]))
+        pair = pair_ref[...].astype(F32).reshape(positions, cz)
+        pair_out_ref[...] = (
+            (pair + tri_gate * update).astype(BF16).reshape(pair_rows, pair_cols, cz)
+        )
+
+    pltpu.make_async_copy(three, three, x_send_sem).wait()
+    wait_all(send, e_send_sem)
+    wait_all(psend, p_send_sem)
+    pltpu.make_async_copy(three, three, o_send_sem).wait()
+    pltpu.make_async_copy(three, three, o_recv_sem).wait()
+
+
+def local_fused(
+    rows,
+    cols,
+    homolog_tensor,
+    pairwise_tensor,
+    genuine_amino_flags,
+    polymer_identity,
+    asking_weights,
+    attend_sigmoid_weights,
+    lookup_content_weights,
+    attend_final_weights,
+    pairwise_logit_weights,
+    crosspolymer_offset,
+    outgoing_link_weights,
+    incoming_link_weights,
+    trimult_sigmoid_weights,
+    trimult_final_weights,
+):
+    count = rows * cols
+    homologs, residues, depth = homolog_tensor.shape
+    pair_rows, pair_cols, cz = pairwise_tensor.shape
+    heads = pairwise_logit_weights.shape[1]
+    total_res = cols * residues
+    seqs = homologs // cols
+    mine = cz // count
+    half = pair_rows * pair_cols // 2
+    row = lax.axis_index("row")
+    flags = genuine_amino_flags.astype(F32)
+    mask = lax.dynamic_slice_in_dim(flags, row * pair_rows, pair_rows, 0)
+    mask = jnp.broadcast_to(mask[:, None], (pair_rows, pair_cols)).reshape(1, -1)
+    cross = (polymer_identity[:, None] != polymer_identity[None, :]).astype(F32)
+    by_owner = jnp.stack(
+        [
+            outgoing_link_weights.reshape(cz, 2, count, mine),
+            incoming_link_weights.reshape(cz, 2, count, mine),
+        ],
+        axis=3,
+    )
+    edge_weights = jnp.concatenate(
+        [
+            jnp.transpose(by_owner, (1, 2, 3, 4, 0)).reshape(4 * cz, cz),
+            jnp.transpose(pairwise_logit_weights),
+            jnp.zeros((16 - heads, cz), BF16),
+        ],
+        axis=0,
+    )
+    final = trimult_final_weights.reshape(count, 1, mine, 1, cz)
+    same_half = jnp.eye(2, dtype=BF16).reshape(1, 2, 1, 2, 1)
+    tri_out = (final * same_half).reshape(count * 2 * mine, 2 * cz)
+    vmem = pl.BlockSpec(memory_space=pltpu.VMEM)
+    smem = pl.BlockSpec(memory_space=pltpu.SMEM)
+    dma = pltpu.SemaphoreType.DMA
+    return pl.pallas_call(
+        functools.partial(fused, (rows, cols, heads, cz)),
+        out_shape=(
+            jax.ShapeDtypeStruct(homolog_tensor.shape, BF16),
+            jax.ShapeDtypeStruct(pairwise_tensor.shape, BF16),
+        ),
+        in_specs=[vmem] * 5 + [smem] + [vmem] * 7,
+        out_specs=(vmem, vmem),
+        scratch_shapes=[
+            pltpu.VMEM((cols, seqs, residues, depth), BF16),
+            pltpu.VMEM((cols, seqs, residues, depth), BF16),
+            pltpu.VMEM((count, 32, half), BF16),
+            pltpu.VMEM((count, 32, half), BF16),
+            pltpu.VMEM((count, 2 * mine, half), F32),
+            pltpu.VMEM((count, 2 * mine, half), F32),
+            pltpu.VMEM((2, 8 * total_res, total_res), F32),
+            pltpu.VMEM((2 * rows, mine, 8, total_res), F32),
+            pltpu.VMEM((heads, total_res, total_res), F32),
+            pltpu.VMEM((pair_rows * pair_cols, cz), BF16),
+        ]
+        + [dma] * 8,
+        compiler_params=pltpu.CompilerParams(
+            collective_id=0, has_side_effects=True, vmem_limit_bytes=40 * 2**20
+        ),
+    )(
+        homolog_tensor,
+        pairwise_tensor,
+        mask,
+        flags.reshape(1, -1),
+        cross,
+        crosspolymer_offset,
+        asking_weights,
+        attend_sigmoid_weights,
+        lookup_content_weights,
+        attend_final_weights,
+        edge_weights,
+        trimult_sigmoid_weights,
+        tri_out,
+    )
 
 
 def from_root(array, axis, root):
@@ -156,4 +530,25 @@
         P(),
     )
     out_specs = (P("row", "col", None), P("row", "col", None))
-    return jax.shard_map(local, mesh=mesh, in_specs=in_specs, out_specs=out_specs, check_vma=False)
+
+    def local_either(*blocks):
+        rows, cols = mesh.shape["row"], mesh.shape["col"]
+        homologs, residues, depth = blocks[0].shape
+        pair_rows, pair_cols, cz = blocks[1].shape
+        heads = blocks[8].shape[1]
+        fits = (
+            cz == 4 * rows * cols
+            and cz == cols * residues
+            and cz == rows * pair_rows
+            and pair_cols == residues == 32
+            and pair_rows == 16
+            and heads == 8
+            and homologs % cols == 0
+            and blocks[4].shape[1] == depth
+            and depth % 128 == 0
+        )
+        if fits:
+            return local_fused(rows, cols, *blocks)
+        return local(*blocks)
+
+    return jax.shard_map(local_either, mesh=mesh, in_specs=in_specs, out_specs=out_specs, check_vma=False)

time: 199 us -> 40.3 us (0.20)
  waiting for transfers between devices: 84.2 us -> 0 us
  blocking collectives: 37.2 us -> 0 us
  Pallas kernels: 0 us -> 33.2 us
  local copies, waits for them, and re-layouts: 32.1 us -> 4.16 us
  matrix products: 19.5 us -> 0 us
  between operations: 14.1 us -> 0.84 us
  other arithmetic: 10.8 us -> 1.9 us
    all_gather x3 -> x0, waiting for transfers between devices: 60.3 us -> none  [the longest x1 40.5 us: local(): left_cols = lax.all_gather(left_tri, 'row', axis=1, tiled=True)]
    all_gather x2 -> x0, blocking collectives: 37.2 us -> none  [the longest x1 31.4 us: local(): all_bias = lax.all_gather(row_bias, 'row', axis=1, tiled=True)]
    pallas_call x0 -> x1, Pallas kernels: none -> 33.2 us  [local_fused(): pl.pallas_call(functools.partial(fused, (rows, cols, heads, cz)), out_sha...]
    psum x1 -> x0, waiting for transfers between devices: 23.2 us -> none  [from_root(): return lax.psum(jnp.where(mine, array, jnp.zeros_like(array)), axis)]
    dot_general x11 -> x0, matrix products: 19.5 us -> none  [the longest x1 3.56 us: local(): jnp.einsum('cki,ckj->cij', left_mine, lax.all_gather(right_tri, 'row', ax...]
    slice x3 -> x0, local copies, waits for them, and re-layouts: 10.7 us -> none  [the longest x2 6.66 us: local(): key_value[..., :inner_width]]
    all_gather x2 -> x0, local copies, waits for them, and re-layouts: 7.46 us -> none  [the longest x1 7.27 us: local(): lax.all_gather(right_tri, 'row', axis=1, tiled=True)]
    reduce_sum x6 -> x0, other arithmetic: 6.78 us -> none  [the longest x1 2.67 us: local(): total_now = total_old * factor + jnp.sum(exp_scores, axis=-1)]
  transfers between devices with their start and end apart: 4 -> 0, of which waited for: 3 -> 0; matrix products, arithmetic and copies ran while one was open for 11% -> 0% of each run, Pallas kernels for 0% -> 0%
where the time goes in v1:
time: 40.3 us; the launch traced here: 40.1 us
  Pallas kernels  33.2 us (82%)
  local copies, waits for them, and re-layouts  4.16 us (10%)
  other arithmetic  1.9 us (5%)
  between operations  0.84 us (2%)
    pallas_call x1, Pallas kernels, local_fused(): pl.pallas_call(functools.partial(fused, (rows, cols, heads, cz)), out_sha...  33.2 us
    unnamed x29, local copies, waits for them, and re-layouts  3.81 us
    convert_element_type x1, other arithmetic, local_fused(): cross = (polymer_identity[:, None] != polymer_identity[None, :]).astype(F32)  0.81 us

profile of v1, /device:TPU:0, one launch (start us, length us, event | category | flops | bytes accessed | tf_op | source)
XLA Modules:
  0.0 40.1 jit_solution(17751994078720408171)
XLA Ops:
  0.6 0.0 copy-start.8
  0.7 0.7 %convert_bitcast_fusion = (f32[1,128]{1,0:T(1,128)S(1)}, f32[128]{0:T(128)S(1)}) fusion(s32[128]{0:T(128)} %param.16), kind=kLoop, calls=%fused_computation.6 | loop fusion | flops 128 | bytes 1536 | tf_op jit(solution)/shard_map/reshape | solution.py:368
  1.3 0.1 dynamic_slice.3
  1.4 0.1 pad.2.clone
  1.5 0.1 broadcast_in_dim.4
  1.6 0.1 reshape.31.mask_ref
  1.7 0.8 %compare_convert_fusion.cross_ref = f32[128,128]{1,0:T(8,128)S(1)} fusion(s32[128]{0:T(128)} %param.17), kind=kLoop, calls=%fused_computation.4 | loop fusion | flops 32768 | bytes 66048 | tf_op jit(solution)/shard_map/convert_element_type | solution.py:318
  2.5 0.0 copy-done.8
  2.5 0.0 copy-start.9
  2.5 0.0 copy-start.10
  2.5 0.1 copy.18
  2.6 0.7 %copy-done.9 = bf16[128,256]{1,0:T(8,128)(2,1)S(1)} copy-done((bf16[128,256]{1,0:T(8,128)(2,1)S(1)}, bf16[128,256]{1,0:T(8,128)(2,1)}, u32[]{:S(2)}) %copy-start.9) | copy-done | bytes 65560
  3.3 0.0 copy-start.5
  3.3 0.1 copy.19
  3.4 0.0 copy-start.11
  3.5 0.0 copy-start.3
  3.5 0.0 copy-start.4
  3.5 0.1 maximum_bitcast_fusion
  3.6 0.0 copy-start
  3.7 0.5 %copy-done.11 = bf16[128,8]{0,1:T(8,128)(2,1)S(1)} copy-done((bf16[128,8]{0,1:T(8,128)(2,1)S(1)}, bf16[128,8]{0,1:T(8,128)(2,1)}, u32[]{:S(2)}) %copy-start.11) | copy-done | bytes 2072
  4.1 0.1 maximum_maximum_fusion.edge_w_ref
  4.3 0.0 copy-done.10
  4.3 0.0 copy-start.1
  4.3 0.2 broadcast_multiply_fusion
  4.5 0.0 copy-start.2
  4.5 0.0 copy-start.6
  4.5 0.0 copy-start.7
  4.5 0.0 copy-done.5
  4.5 0.0 copy-done.3
  4.6 0.0 copy-done.4
  4.6 0.1 copy-done
  4.7 0.6 %copy-done.1 = bf16[256,512]{1,0:T(8,128)(2,1)S(1)} copy-done((bf16[256,512]{1,0:T(8,128)(2,1)S(1)}, bf16[256,512]{1,0:T(8,128)(2,1)}, u32[]{:S(2)}) %copy-start.1) | copy-done | bytes 262168
  5.3 0.1 copy-done.2
  5.4 0.0 copy-done.6
  5.4 0.0 copy-done.7
  5.4 33.2 %shard_map.149 = (bf16[32,32,256]{2,1,0:T(8,128)(2,1)S(1)}, bf16[16,32,128]{2,1,0:T(8,128)(2,1)S(1)}) custom-call(bf16[32,32,256]{2,1,0:T(8,128)(2,1)S(1)} %copy-done, bf16[16,32,128]{2,1,0:T(8,128)(2,1)S(1)} %copy-done.2, f32[1,512]{1,0:T(1,128)S(1)} %reshape.31.mask_ref, f32[1,128]{1,0:T(1,128)S(1)} %get-tuple-element.2.keep_ref, ...), custom_call_target="tpu_custom_call" | custom-call | tf_op jit(solution)/shard_map/pallas_call | solution.py:340
  38.6 0.8 %copy.26 = bf16[32,32,256]{2,1,0:T(8,128)(2,1)} copy(bf16[32,32,256]{2,1,0:T(8,128)(2,1)S(1)} %get-tuple-element.6) | data formatting | bytes 1048576
  39.4 0.7 %copy.27 = bf16[16,32,128]{2,1,0:T(8,128)(2,1)} copy(bf16[16,32,128]{2,1,0:T(8,128)(2,1)S(1)} %get-tuple-element.7) | data formatting | bytes 262144
  (4 shorter events, 0.1 us)
Async XLA Ops:
  0.6 1.8 %copy-start.8 = (bf16[128,256]{1,0:T(8,128)(2,1)S(1)}, bf16[128,256]{1,0:T(8,128)(2,1)}, u32[]{:S(2)}) copy-start(bf16[128,256]{1,0:T(8,128)(2,1)} %param.24) | copy-start | bytes 196612
  2.5 0.8 %copy-start.9 = (bf16[128,256]{1,0:T(8,128)(2,1)S(1)}, bf16[128,256]{1,0:T(8,128)(2,1)}, u32[]{:S(2)}) copy-start(bf16[128,256]{1,0:T(8,128)(2,1)} %param.25) | copy-start | bytes 196612
  2.5 1.8 %copy-start.10 = (bf16[128,128]{1,0:T(8,128)(2,1)S(1)}, bf16[128,128]{1,0:T(8,128)(2,1)}, u32[]{:S(2)}) copy-start(bf16[128,128]{1,0:T(8,128)(2,1)} %param.27) | copy-start | bytes 98308
  3.3 1.2 %copy-start.5 = (bf16[256,256]{1,0:T(8,128)(2,1)S(1)}, bf16[256,256]{1,0:T(8,128)(2,1)}, u32[]{:S(2)}) copy-start(bf16[256,256]{1,0:T(8,128)(2,1)} %wo_ref.1) | copy-start | bytes 393220
  3.4 0.7 %copy-start.11 = (bf16[128,8]{0,1:T(8,128)(2,1)S(1)}, bf16[128,8]{0,1:T(8,128)(2,1)}, u32[]{:S(2)}) copy-start(bf16[128,8]{0,1:T(8,128)(2,1)} %param.22) | copy-start | bytes 6148
  3.5 1.1 %copy-start.3 = (bf16[256,256]{1,0:T(8,128)(2,1)S(1)}, bf16[256,256]{1,0:T(8,128)(2,1)}, u32[]{:S(2)}) copy-start(bf16[256,256]{1,0:T(8,128)(2,1)} %wq_ref.1) | copy-start | bytes 393220
  3.5 1.1 %copy-start.4 = (bf16[256,256]{1,0:T(8,128)(2,1)S(1)}, bf16[256,256]{1,0:T(8,128)(2,1)}, u32[]{:S(2)}) copy-start(bf16[256,256]{1,0:T(8,128)(2,1)} %wg_ref.1) | copy-start | bytes 393220
  3.6 1.1 %copy-start = (bf16[32,32,256]{2,1,0:T(8,128)(2,1)S(1)}, bf16[32,32,256]{2,1,0:T(8,128)(2,1)}, u32[]{:S(2)}) copy-start(bf16[32,32,256]{2,1,0:T(8,128)(2,1)} %x_ref.1) | copy-start | bytes 1572868
  4.3 1.0 %copy-start.1 = (bf16[256,512]{1,0:T(8,128)(2,1)S(1)}, bf16[256,512]{1,0:T(8,128)(2,1)}, u32[]{:S(2)}) copy-start(bf16[256,512]{1,0:T(8,128)(2,1)} %wkv_ref.1) | copy-start | bytes 786436
  4.5 1.0 %copy-start.2 = (bf16[16,32,128]{2,1,0:T(8,128)(2,1)S(1)}, bf16[16,32,128]{2,1,0:T(8,128)(2,1)}, u32[]{:S(2)}) copy-start(bf16[16,32,128]{2,1,0:T(8,128)(2,1)} %pair_ref.1) | copy-start | bytes 393220
  4.5 1.0 %copy-start.6 = (bf16[128,128]{1,0:T(8,128)(2,1)S(1)}, bf16[128,128]{1,0:T(8,128)(2,1)}, u32[]{:S(2)}) copy-start(bf16[128,128]{1,0:T(8,128)(2,1)} %tri_gate_w_ref.1) | copy-start | bytes 98308
  4.5 0.9 %copy-start.7 = (f32[8]{0:T(128)S(1)}, f32[8]{0:T(128)}, u32[]{:S(2)}) copy-start(f32[8]{0:T(128)} %offset_ref.1) | copy-start | bytes 100

commit v2 on v1

--- a/solution.py
+++ b/solution.py
@@ -34,30 +34,48 @@
 def fused(
     dims,
     x_ref,
-    pair_ref,
-    mask_ref,
+    pair_hbm,
+    flags_smem,
     keep_ref,
-    cross_ref,
+    identity_ref,
     offset_ref,
-    wq_ref,
-    wg_ref,
-    wkv_ref,
-    wo_ref,
-    edge_w_ref,
-    tri_gate_w_ref,
-    tri_out_w_ref,
+    wq_hbm,
+    wg_hbm,
+    wkv_hbm,
+    wo_hbm,
+    bias_w_ref,
+    left_w_hbm,
+    right_w_hbm,
+    tri_gate_w_hbm,
+    tri_out_w_hbm,
     msa_out_ref,
     pair_out_ref,
     hx,
     hout,
     send,
     recv,
+    brecv,
     psend,
     precv,
     zed,
     zprod,
     extra,
     pn_ref,
+    q_ref,
+    k_ref,
+    v_ref,
+    g_ref,
+    pair_ref,
+    wq_ref,
+    wg_ref,
+    wkv_ref,
+    wo_ref,
+    left_w_ref,
+    right_w_ref,
+    tri_gate_w_ref,
+    tri_out_w_ref,
+    in_sem,
+    own_sem,
     x_send_sem,
     x_recv_sem,
     e_send_sem,
@@ -66,9 +84,14 @@
     p_recv_sem,
     o_send_sem,
     o_recv_sem,
+    r_send_sem,
+    r_recv_sem,
+    c_send_sem,
+    c_recv_sem,
 ):
     rows, cols, heads, channels = dims
     count = rows * cols
+    mine = channels // count
     row = lax.axis_index("row")
     col = lax.axis_index("col")
     me = row * cols + col
@@ -77,6 +100,8 @@
     width = depth // heads
     pair_rows, pair_cols, cz = pair_ref.shape
     positions = pair_rows * pair_cols
+    half = positions // 2
+    both = 2 * cz
 
     def other(step):
         peer = lax.rem(me + step, count)
@@ -88,36 +113,78 @@
         pl.semaphore_signal(barrier, inc=1, device_id=other(step), device_id_type=MESH)
         return carry
 
+    loads = [
+        pltpu.make_async_copy(source, target, in_sem.at[n])
+        for n, (source, target) in enumerate(
+            (
+                (pair_hbm, pair_ref),
+                (left_w_hbm, left_w_ref),
+                (right_w_hbm, right_w_ref),
+                (tri_out_w_hbm, tri_out_w_ref),
+                (tri_gate_w_hbm, tri_gate_w_ref),
+                (wq_hbm, wq_ref),
+                (wkv_hbm, wkv_ref),
+                (wg_hbm, wg_ref),
+                (wo_hbm, wo_ref),
+            )
+        )
+    ]
+    for load in loads:
+        load.start()
+    own = pltpu.make_async_copy(x_ref.at[pl.ds(col * seqs, seqs)], hx.at[col], own_sem)
+    own.start()
     lax.fori_loop(1, count, greet, 0)
-    pl.semaphore_wait(barrier, count - 1)
-
-    for step in range(1, cols):
-        peer = lax.rem(col + step, cols)
-        pltpu.make_async_remote_copy(
-            src_ref=x_ref.at[pl.ds(peer * seqs, seqs)],
-            dst_ref=hx.at[col],
-            send_sem=x_send_sem,
-            recv_sem=x_recv_sem,
-            device_id=(row, peer),
-            device_id_type=MESH,
-        ).start()
-    hx[pl.ds(col, 1)] = x_ref[pl.ds(col * seqs, seqs)][None]
+
+    with jax.named_scope("weights_by_owner"):
+        to = lax.broadcasted_iota(jnp.int32, (both, both), 0)
+        source = lax.broadcasted_iota(jnp.int32, (both, both), 1)
+        wanted = (to % (2 * mine)) // mine * cz + to // (2 * mine) * mine + to % mine
+        order = (source == wanted).astype(BF16)
+        loads[1].wait()
+        loads[2].wait()
+        edge_w = [
+            dot(
+                order,
+                jnp.concatenate(
+                    [left_w_ref[:, n * cz : n * cz + cz], right_w_ref[:, n * cz : n * cz + cz]],
+                    axis=1,
+                ),
+                ((1,), (1,)),
+            ).astype(BF16)
+            for n in range(2)
+        ]
 
     with jax.named_scope("pair_edges_and_bias"):
+        loads[0].wait()
         pair = pair_ref[...].astype(F32).reshape(positions, cz)
         pn = normalize(pair, -1).astype(BF16)
         pn_ref[...] = pn
-        proj = dot(edge_w_ref[...], pn, ((1,), (1,)))
-        both = 2 * cz
-        edge = mask_ref[...] * jax.nn.sigmoid(proj[:both]) * proj[both : 2 * both]
-        half = positions // 2
-        edge = edge.reshape(count, 8, positions)
-        bias = proj[2 * both : 2 * both + 8]
-        send[:, :16, :] = jnp.concatenate(
-            [edge[:, :, :half], edge[:, :, half:]], axis=1
-        ).astype(BF16)
+        bias = dot(bias_w_ref[...], pn, ((1,), (1,)))
         bias = jnp.concatenate([bias[:, :half], bias[:, half:]], axis=0).astype(BF16)
-        send[:, 16:, :] = jnp.broadcast_to(bias[None], (count, 16, half))
+        brecv[pl.ds(col * rows + row, 1)] = bias[None]
+        k_of = lane_blocks((1, positions), pair_cols)
+        mask = jnp.zeros((1, positions), F32)
+        for k in range(pair_rows):
+            mask = jnp.where(k_of == k, flags_smem[row * pair_rows + k].astype(F32), mask)
+        edge = (
+            mask
+            * jax.nn.sigmoid(dot(edge_w[0], pn, ((1,), (1,))))
+            * dot(edge_w[1], pn, ((1,), (1,)))
+        )
+        edge = edge.reshape(count, 2 * mine, positions)
+        send[...] = jnp.concatenate([edge[:, :, :half], edge[:, :, half:]], axis=1).astype(BF16)
+
+    pl.semaphore_wait(barrier, count - 1)
+
+    for step in range(1, rows):
+        pltpu.make_async_remote_copy(
+            src_ref=brecv.at[col * rows + row],
+            dst_ref=brecv.at[col * rows + row],
+            send_sem=r_send_sem,
+            recv_sem=r_recv_sem,
+            device_id=(lax.rem(row + step, rows), col),
+            device_id_type=MESH,
+        ).start()
 
     def push(step, carry):
         to_row, to_col = other(step)
@@ -133,37 +200,84 @@
         return carry
 
     lax.fori_loop(1, count, push, 0)
+    for step in range(1, cols):
+        peer = lax.rem(col + step, cols)
+        pltpu.make_async_remote_copy(
+            src_ref=x_ref.at[pl.ds(peer * seqs, seqs)],
+            dst_ref=hx.at[col],
+            send_sem=x_send_sem,
+            recv_sem=x_recv_sem,
+            device_id=(row, peer),
+            device_id_type=MESH,
+        ).start()
     recv[pl.ds(me, 1)] = send[pl.ds(me, 1)]
 
-    def wait_all(ref, sem):
-        part = ref.at[pl.ds(0, count - 1)]
+    def wait_for(ref, number, sem):
+        part = ref.at[pl.ds(0, number)]
         pltpu.make_async_copy(part, part, sem).wait()
 
-    wait_all(recv, e_recv_sem)
+    wait_for(brecv, rows - 1, r_recv_sem)
+    for step in range(1, cols):
+        pltpu.make_async_remote_copy(
+            src_ref=brecv.at[pl.ds(col * rows, rows)],
+            dst_ref=brecv.at[pl.ds(col * rows, rows)],
+            send_sem=c_send_sem,
+            recv_sem=c_recv_sem,
+            device_id=(row, lax.rem(col + step, cols)),
+            device_id_type=MESH,
+        ).start()
+
+    own.wait()
+    wait_for(hx, cols - 1, x_recv_sem)
+    for load in loads[5:]:
+        load.wait()
+    with jax.named_scope("projections"):
+        for c in range(cols):
+            shape = (seqs, residues, depth)
+            x = hx[c].reshape(seqs * residues, depth).astype(F32)
+            xn = normalize(x, -1).astype(BF16)
+            queries = dot(xn, wq_ref[...]) * width ** (-0.5)
+            q_ref[c] = queries.astype(BF16).reshape(shape)
+            kv = dot(xn, wkv_ref[...]).astype(BF16)
+            k_ref[c] = kv[:, :depth].reshape(shape)
+            v_ref[c] = kv[:, depth:].reshape(shape)
+            g_ref[c] = jax.nn.sigmoid(dot(xn, wg_ref[...])).reshape(shape)
+
+    wait_for(recv, count - 1, e_recv_sem)
 
     block = pair_cols
     lanes = total_res
     per_tile = lanes // block
     where_block = lane_blocks((16 * rows, lanes), block)
-    with jax.named_scope("to_matrices"):
-        for part in range(2):
-            for tile in range(half // lanes):
-                taken = recv[:, part * 16 : part * 16 + 16, tile * lanes : (tile + 1) * lanes]
-                taken = taken.astype(F32).reshape(rows, cols, 16, lanes)
-                pieces = [taken[:, c].reshape(16 * rows, lanes) for c in range(cols)]
-                for k in range(per_tile):
-                    merged = shift_lanes(pieces[0], (0 - k) * block)
-                    for c in range(1, cols):
-                        merged = jnp.where(
-                            where_block == c, shift_lanes(pieces[c], (c - k) * block), merged
-                        )
-                    zed[part, pl.ds(tile * per_tile + k, 16 * rows, stride=8), :] = merged
+
+    def to_matrices(part, pieces_of):
+        for tile in range(half // lanes):
+            pieces = pieces_of(tile)
+            for k in range(per_tile):
+                merged = shift_lanes(pieces[0], (0 - k) * block)
+                for c in range(1, cols):
+                    merged = jnp.where(
+                        where_block == c, shift_lanes(pieces[c], (c - k) * block), merged
+                    )
+                zed[part, pl.ds(tile * per_tile + k, 16 * rows, stride=8), :] = merged
+
+    def edge_pieces(tile):
+        taken = recv[:, :, tile * lanes : (tile + 1) * lanes]
+        taken = taken.astype(F32).reshape(rows, cols, 16, lanes)
+        return [taken[:, c].reshape(16 * rows, lanes) for c in range(cols)]
+
+    def bias_pieces(tile):
+        taken = brecv[:, :, tile * lanes : (tile + 1) * lanes]
+        taken = taken.astype(F32).reshape(cols, 16 * rows, lanes)
+        return [taken[c] for c in range(cols)]
+
+    with jax.named_scope("edge_matrices"):
+        to_matrices(0, edge_pieces)
 
     def matrix(part, q):
         return zed[part].reshape(2 * rows, 8, 8, lanes)[:, q].reshape(total_res, lanes)
 
     with jax.named_scope("triangle_product"):
-        mine = channels // count
         for ch in range(mine):
             left = matrix(0, ch).T.astype(BF16)
             right = matrix(0, mine + ch).astype(BF16)
@@ -205,29 +319,25 @@
     lax.fori_loop(1, count, push_product, 0)
     precv[pl.ds(me, 1)] = psend[pl.ds(me, 1)]
 
+    wait_for(brecv, (cols - 1) * rows, c_recv_sem)
     with jax.named_scope("attention_bias"):
+        to_matrices(1, bias_pieces)
+        identity = jnp.broadcast_to(identity_ref[...].astype(F32), (total_res, total_res))
+        cross = (identity.T != identity).astype(F32)
         for h in range(heads):
-            extra[h] = matrix(1, h) + offset_ref[h] * cross_ref[...]
-
-    three = hx.at[pl.ds(0, cols - 1)]
-    pltpu.make_async_copy(three, three, x_recv_sem).wait()
+            extra[h] = matrix(1, h) + offset_ref[h] * cross
 
     keep = keep_ref[...] > 0
     head_of = lane_blocks((total_res, depth), width)
-
-    def attend(s, carry):
-        x = hx[:, s].reshape(total_res, depth).astype(F32)
-        xn = normalize(x, -1).astype(BF16)
-        queries = (dot(xn, wq_ref[...]) * width ** (-0.5)).astype(BF16)
-        kv = dot(xn, wkv_ref[...])
-        keys, values = kv[:, :depth], kv[:, depth:]
-        gate = jax.nn.sigmoid(dot(xn, wg_ref[...]))
-        key_stack = jnp.concatenate(
-            [jnp.where(head_of == h, keys, 0.0).astype(BF16) for h in range(heads)], axis=0
-        )
-        value_stack = jnp.concatenate(
-            [jnp.where(head_of == h, values, 0.0).astype(BF16) for h in range(heads)], axis=0
-        )
+    in_head = [(lane_blocks((1, depth), width) == h).astype(F32).astype(BF16) for h in range(heads)]
+    at_once = 2 if seqs % 2 == 0 else 1
+
+    def attend(s):
+        queries = q_ref[:, s].reshape(total_res, depth)
+        keys = k_ref[:, s].reshape(total_res, depth)
+        values = v_ref[:, s].reshape(total_res, depth)
+        key_stack = jnp.concatenate([keys * in_head[h] for h in range(heads)], axis=0)
+        value_stack = jnp.concatenate([values * in_head[h] for h in range(heads)], axis=0)
         scores = dot(queries, key_stack, ((1,), (1,)))
         probs = []
         total = jnp.ones((total_res, depth), F32)
@@ -238,26 +348,36 @@
             total = jnp.where(head_of == h, jnp.sum(one, axis=-1, keepdims=True), total)
             probs.append(one.astype(BF16))
         attended = dot(jnp.concatenate(probs, axis=1), value_stack) / total
+        gate = g_ref[:, s].reshape(total_res, depth)
         gated = (gate * attended).astype(BF16)
+        x = hx[:, s].reshape(total_res, depth).astype(F32)
         result = (x + dot(gated, wo_ref[...])).astype(BF16)
-        hout[:, s] = result.reshape(cols, residues, depth)
+        return result.reshape(cols, residues, depth)
+
+    def attend_group(group, carry):
+        first = group * at_once
+        results = [attend(first + n) for n in range(at_once)]
+        for n in range(at_once):
+            hout[:, first + n] = results[n]
         for step in range(1, cols):
             peer = lax.rem(col + step, cols)
             pltpu.make_async_remote_copy(
-                src_ref=hout.at[peer, s],
-                dst_ref=msa_out_ref.at[col * seqs + s],
+                src_ref=hout.at[peer, pl.ds(first, at_once)],
+                dst_ref=msa_out_ref.at[pl.ds(col * seqs + first, at_once)],
                 send_sem=o_send_sem,
                 recv_sem=o_recv_sem,
                 device_id=(row, peer),
                 device_id_type=MESH,
             ).start()
-        msa_out_ref[pl.ds(col * seqs + s, 1)] = hout[pl.ds(col, 1), s]
+        msa_out_ref[pl.ds(col * seqs + first, at_once)] = hout[col, pl.ds(first, at_once)]
         return carry
 
     with jax.named_scope("row_attention"):
-        lax.fori_loop(0, seqs, attend, 0)
-
-    wait_all(precv, p_recv_sem)
+        lax.fori_loop(0, seqs // at_once, attend_group, 0)
+
+    wait_for(precv, count - 1, p_recv_sem)
+    loads[3].wait()
+    loads[4].wait()
     with jax.named_scope("pair_update"):
         product = precv[...]
         in_half = lax.broadcasted_iota(jnp.int32, (8, half), 0) < mine
@@ -270,7 +390,15 @@
         center = product - spread_halves(jnp.sum(product, axis=0))[None]
         spread = spread_halves(jnp.sum(center * center, axis=0))
         norm = (center * lax.rsqrt(spread + 1e-05)[None]).reshape(count * 8, half)
-        update = dot(norm.T.astype(BF16), tri_out_w_ref[...])
+        to = lax.broadcasted_iota(jnp.int32, (2 * channels, channels), 0)
+        source = lax.broadcasted_iota(jnp.int32, (2 * channels, channels), 1)
+        wanted = to // (2 * mine) * mine + to % mine
+        final_w = dot((source == wanted).astype(BF16), tri_out_w_ref[...])
+        low_rows = to % (2 * mine) < mine
+        final_w = jnp.concatenate(
+            [jnp.where(low_rows, final_w, 0.0), jnp.where(low_rows, 0.0, final_w)], axis=1
+        ).astype(BF16)
+        update = dot(norm.T.astype(BF16), final_w)
         update = jnp.concatenate([update[:, :cz], update[:, cz:]], axis=0)
         tri_gate = jax.nn.sigmoid(dot(pn_ref[...], tri_gate_w_ref[...]))
         pair = pair_ref[...].astype(F32).reshape(positions, cz)
@@ -278,11 +406,13 @@
             (pair + tri_gate * update).astype(BF16).reshape(pair_rows, pair_cols, cz)
         )
 
-    pltpu.make_async_copy(three, three, x_send_sem).wait()
-    wait_all(send, e_send_sem)
-    wait_all(psend, p_send_sem)
-    pltpu.make_async_copy(three, three, o_send_sem).wait()
-    pltpu.make_async_copy(three, three, o_recv_sem).wait()
+    wait_for(hx, cols - 1, x_send_sem)
+    wait_for(send, count - 1, e_send_sem)
+    wait_for(psend, count - 1, p_send_sem)
+    wait_for(brecv, rows - 1, r_send_sem)
+    wait_for(brecv, (cols - 1) * rows, c_send_sem)
+    wait_for(hout, cols - 1, o_send_sem)
+    wait_for(hout, cols - 1, o_recv_sem)
 
 
 def local_fused(
@@ -311,70 +441,66 @@
     seqs = homologs // cols
     mine = cz // count
     half = pair_rows * pair_cols // 2
-    row = lax.axis_index("row")
-    flags = genuine_amino_flags.astype(F32)
-    mask = lax.dynamic_slice_in_dim(flags, row * pair_rows, pair_rows, 0)
-    mask = jnp.broadcast_to(mask[:, None], (pair_rows, pair_cols)).reshape(1, -1)
-    cross = (polymer_identity[:, None] != polymer_identity[None, :]).astype(F32)
-    by_owner = jnp.stack(
-        [
-            outgoing_link_weights.reshape(cz, 2, count, mine),
-            incoming_link_weights.reshape(cz, 2, count, mine),
-        ],
-        axis=3,
-    )
-    edge_weights = jnp.concatenate(
-        [
-            jnp.transpose(by_owner, (1, 2, 3, 4, 0)).reshape(4 * cz, cz),
-            jnp.transpose(pairwise_logit_weights),
-            jnp.zeros((16 - heads, cz), BF16),
-        ],
-        axis=0,
-    )
-    final = trimult_final_weights.reshape(count, 1, mine, 1, cz)
-    same_half = jnp.eye(2, dtype=BF16).reshape(1, 2, 1, 2, 1)
-    tri_out = (final * same_half).reshape(count * 2 * mine, 2 * cz)
     vmem = pl.BlockSpec(memory_space=pltpu.VMEM)
     smem = pl.BlockSpec(memory_space=pltpu.SMEM)
+    hbm = pl.BlockSpec(memory_space=pltpu.HBM)
     dma = pltpu.SemaphoreType.DMA
+    msa_block = (cols, seqs, residues, depth)
     return pl.pallas_call(
         functools.partial(fused, (rows, cols, heads, cz)),
         out_shape=(
             jax.ShapeDtypeStruct(homolog_tensor.shape, BF16),
             jax.ShapeDtypeStruct(pairwise_tensor.shape, BF16),
         ),
-        in_specs=[vmem] * 5 + [smem] + [vmem] * 7,
+        in_specs=[hbm, hbm, smem, vmem, vmem, smem] + [hbm] * 4 + [vmem] + [hbm] * 4,
         out_specs=(vmem, vmem),
         scratch_shapes=[
-            pltpu.VMEM((cols, seqs, residues, depth), BF16),
-            pltpu.VMEM((cols, seqs, residues, depth), BF16),
-            pltpu.VMEM((count, 32, half), BF16),
-            pltpu.VMEM((count, 32, half), BF16),
+            pltpu.VMEM(msa_block, BF16),
+            pltpu.VMEM(msa_block, BF16),
+            pltpu.VMEM((count, 16, half), BF16),
+            pltpu.VMEM((count, 16, half), BF16),
+            pltpu.VMEM((count, 16, half), BF16),
             pltpu.VMEM((count, 2 * mine, half), F32),
             pltpu.VMEM((count, 2 * mine, half), F32),
             pltpu.VMEM((2, 8 * total_res, total_res), F32),
             pltpu.VMEM((2 * rows, mine, 8, total_res), F32),
             pltpu.VMEM((heads, total_res, total_res), F32),
             pltpu.VMEM((pair_rows * pair_cols, cz), BF16),
+            pltpu.VMEM(msa_block, BF16),
+            pltpu.VMEM(msa_block, BF16),
+            pltpu.VMEM(msa_block, BF16),
+            pltpu.VMEM(msa_block, F32),
+            pltpu.VMEM((pair_rows, pair_cols, cz), BF16),
+            pltpu.VMEM(asking_weights.shape, BF16),
+            pltpu.VMEM(attend_sigmoid_weights.shape, BF16),
+            pltpu.VMEM(lookup_content_weights.shape, BF16),
+            pltpu.VMEM(attend_final_weights.shape, BF16),
+            pltpu.VMEM(outgoing_link_weights.shape, BF16),
+            pltpu.VMEM(incoming_link_weights.shape, BF16),
+            pltpu.VMEM(trimult_sigmoid_weights.shape, BF16),
+            pltpu.VMEM(trimult_final_weights.shape, BF16),
+            dma((9,)),
         ]
-        + [dma] * 8,
+        + [dma] * 13,
         compiler_params=pltpu.CompilerParams(
-            collective_id=0, has_side_effects=True, vmem_limit_bytes=40 * 2**20
+            collective_id=0, has_side_effects=True, vmem_limit_bytes=62 * 2**20
         ),
     )(
         homolog_tensor,
         pairwise_tensor,
-        mask,
-        flags.reshape(1, -1),
-        cross,
+        genuine_amino_flags,
+        genuine_amino_flags.reshape(1, -1),
+        polymer_identity.reshape(1, -1),
         crosspolymer_offset,
         asking_weights,
         attend_sigmoid_weights,
         lookup_content_weights,
         attend_final_weights,
-        edge_weights,
+        jnp.transpose(pairwise_logit_weights),
+        outgoing_link_weights,
+        incoming_link_weights,
         trimult_sigmoid_weights,
-        tri_out,
+        trimult_final_weights,
     )
 
 

time: 40.3 us -> 34.8 us (0.86)
  other arithmetic: 1.9 us -> 0 us
  Pallas kernels: 33.2 us -> 31.4 us
  local copies, waits for them, and re-layouts: 4.16 us -> 2.56 us
    pallas_call x1, Pallas kernels: 33.2 us -> 31.4 us  [local_fused(): pl.pallas_call(functools.partial(fused, (rows, cols, heads, cz)), out_sha...]
    unnamed x29 -> x4, local copies, waits for them, and re-layouts: 3.81 us -> 2.56 us
    convert_element_type x2 -> x0, other arithmetic: 0.82 us -> none  [the longest x1 0.81 us: local_fused(): cross = (polymer_identity[:, None] != polymer_identity[None, :]).astype(F32)]
    reshape x1 -> x0, other arithmetic: 0.69 us -> none  [local_fused(): flags.reshape(1, -1)]
where the time goes in v2:
time: 34.8 us; the launch traced here: 34.6 us
  Pallas kernels  31.4 us (90%)
  local copies, waits for them, and re-layouts  2.56 us (7%)
  between operations  0.65 us (2%)
    pallas_call x1, Pallas kernels, local_fused(): pl.pallas_call(functools.partial(fused, (rows, cols, heads, cz)), out_sha...  31.4 us
    unnamed x4, local copies, waits for them, and re-layouts  2.56 us

profile of v2, /device:TPU:0, one launch (start us, length us, event | category | flops | bytes accessed | tf_op | source)
XLA Modules:
  0.0 34.6 jit_solution(9959534059729595160)
XLA Ops:
  0.6 31.4 %shard_map.149 = (bf16[32,32,256]{2,1,0:T(8,128)(2,1)}, bf16[16,32,128]{2,1,0:T(8,128)(2,1)}) custom-call(bf16[32,32,256]{2,1,0:T(8,128)(2,1)} %x_ref.1, bf16[16,32,128]{2,1,0:T(8,128)(2,1)} %pair_hbm.1, s32[128]{0:T(128)} %flags_smem.1, s32[1,128]{1,0:T(1,128)} %bitcast.4, s32[1,128]{1,0:T(1,128)} %bitcast.5, f32[8]{0:T(128)} %offset_ref.1, ...), custom_call_target="tpu_custom_call" | custom-call | tf_op jit(solution)/shard_map/pallas_call | solution.py:449
  32.1 0.0 copy-start
  32.1 1.9 %copy.18 = bf16[32,32,256]{2,1,0:T(8,128)(2,1)} copy(bf16[32,32,256]{2,1,0:T(8,128)(2,1)} %get-tuple-element.4) | data formatting | bytes 1048576
  34.0 0.0 copy-done
  34.0 0.7 %copy.19 = bf16[16,32,128]{2,1,0:T(8,128)(2,1)} copy(bf16[16,32,128]{2,1,0:T(8,128)(2,1)S(1)} %copy-done) | data formatting | bytes 262144
Async XLA Ops:
  32.1 1.9 %copy-start = (bf16[16,32,128]{2,1,0:T(8,128)(2,1)S(1)}, bf16[16,32,128]{2,1,0:T(8,128)(2,1)}, u32[]{:S(2)}) copy-start(bf16[16,32,128]{2,1,0:T(8,128)(2,1)} %get-tuple-element.5) | copy-start | bytes 393220

commit v3 on v2

--- a/solution.py
+++ b/solution.py
@@ -154,7 +154,19 @@
             for n in range(2)
         ]
 
-    with jax.named_scope("pair_edges_and_bias"):
+    pl.semaphore_wait(barrier, count - 1)
+    for step in range(1, cols):
+        peer = lax.rem(col + step, cols)
+        pltpu.make_async_remote_copy(
+            src_ref=x_ref.at[pl.ds(peer * seqs, seqs)],
+            dst_ref=hx.at[col],
+            send_sem=x_send_sem,
+            recv_sem=x_recv_sem,
+            device_id=(row, peer),
+            device_id_type=MESH,
+        ).start()
+
+    with jax.named_scope("pair_bias"):
         loads[0].wait()
         pair = pair_ref[...].astype(F32).reshape(positions, cz)
         pn = normalize(pair, -1).astype(BF16)
@@ -162,6 +174,18 @@
         bias = dot(bias_w_ref[...], pn, ((1,), (1,)))
         bias = jnp.concatenate([bias[:, :half], bias[:, half:]], axis=0).astype(BF16)
         brecv[pl.ds(col * rows + row, 1)] = bias[None]
+
+    for step in range(1, rows):
+        pltpu.make_async_remote_copy(
+            src_ref=brecv.at[col * rows + row],
+            dst_ref=brecv.at[col * rows + row],
+            send_sem=r_send_sem,
+            recv_sem=r_recv_sem,
+            device_id=(lax.rem(row + step, rows), col),
+            device_id_type=MESH,
+        ).start()
+
+    with jax.named_scope("pair_edges"):
         k_of = lane_blocks((1, positions), pair_cols)
         mask = jnp.zeros((1, positions), F32)
         for k in range(pair_rows):
@@ -174,15 +198,20 @@
         edge = edge.reshape(count, 2 * mine, positions)
         send[...] = jnp.concatenate([edge[:, :, :half], edge[:, :, half:]], axis=1).astype(BF16)
 
-    pl.semaphore_wait(barrier, count - 1)
-
-    for step in range(1, rows):
+    recv[pl.ds(me, 1)] = send[pl.ds(me, 1)]
+
+    def wait_for(ref, number, sem):
+        part = ref.at[pl.ds(0, number)]
+        pltpu.make_async_copy(part, part, sem).wait()
+
+    wait_for(brecv, rows - 1, r_recv_sem)
+    for step in range(1, cols):
         pltpu.make_async_remote_copy(
-            src_ref=brecv.at[col * rows + row],
-            dst_ref=brecv.at[col * rows + row],
-            send_sem=r_send_sem,
-            recv_sem=r_recv_sem,
-            device_id=(lax.rem(row + step, rows), col),
+            src_ref=brecv.at[pl.ds(col * rows, rows)],
+            dst_ref=brecv.at[pl.ds(col * rows, rows)],
+            send_sem=c_send_sem,
+            recv_sem=c_recv_sem,
+            device_id=(row, lax.rem(col + step, cols)),
             device_id_type=MESH,
         ).start()
 
@@ -200,33 +229,6 @@
         return carry
 
     lax.fori_loop(1, count, push, 0)
-    for step in range(1, cols):
-        peer = lax.rem(col + step, cols)
-        pltpu.make_async_remote_copy(
-            src_ref=x_ref.at[pl.ds(peer * seqs, seqs)],
-            dst_ref=hx.at[col],
-            send_sem=x_send_sem,
-            recv_sem=x_recv_sem,
-            device_id=(row, peer),
-            device_id_type=MESH,
-        ).start()
-    recv[pl.ds(me, 1)] = send[pl.ds(me, 1)]
-
-    def wait_for(ref, number, sem):
-        part = ref.at[pl.ds(0, number)]
-        pltpu.make_async_copy(part, part, sem).wait()
-
-    wait_for(brecv, rows - 1, r_recv_sem)
-    for step in range(1, cols):
-        pltpu.make_async_remote_copy(
-            src_ref=brecv.at[pl.ds(col * rows, rows)],
-            dst_ref=brecv.at[pl.ds(col * rows, rows)],
-            send_sem=c_send_sem,
-            recv_sem=c_recv_sem,
-            device_id=(row, lax.rem(col + step, cols)),
-            device_id_type=MESH,
-        ).start()
-
     own.wait()
     wait_for(hx, cols - 1, x_recv_sem)
     for load in loads[5:]:
@@ -243,8 +245,6 @@
             v_ref[c] = kv[:, depth:].reshape(shape)
             g_ref[c] = jax.nn.sigmoid(dot(xn, wg_ref[...])).reshape(shape)
 
-    wait_for(recv, count - 1, e_recv_sem)
-
     block = pair_cols
     lanes = total_res
     per_tile = lanes // block
@@ -271,12 +271,72 @@
         taken = taken.astype(F32).reshape(cols, 16 * rows, lanes)
         return [taken[c] for c in range(cols)]
 
+    def matrix(part, q):
+        return zed[part].reshape(2 * rows, 8, 8, lanes)[:, q].reshape(total_res, lanes)
+
+    wait_for(brecv, (cols - 1) * rows, c_recv_sem)
+    with jax.named_scope("attention_bias"):
+        to_matrices(1, bias_pieces)
+        identity = jnp.broadcast_to(identity_ref[...].astype(F32), (total_res, total_res))
+        cross = (identity.T != identity).astype(F32)
+        for h in range(heads):
+            extra[h] = matrix(1, h) + offset_ref[h] * cross
+
+    keep = keep_ref[...] > 0
+    head_of = lane_blocks((total_res, 128), width)
+    in_head = [(lane_blocks((1, depth), width) == h).astype(F32).astype(BF16) for h in range(heads)]
+    at_once = 2 if seqs % 2 == 0 else 1
+
+    def attend(s):
+        queries = q_ref[:, s].reshape(total_res, depth)
+        keys = k_ref[:, s].reshape(total_res, depth)
+        values = v_ref[:, s].reshape(total_res, depth)
+        key_stack = jnp.concatenate([keys * in_head[h] for h in range(heads)], axis=0)
+        value_stack = jnp.concatenate([values * in_head[h] for h in range(heads)], axis=0)
+        scores = dot(queries, key_stack, ((1,), (1,)))
+        probs = []
+        totals = [jnp.ones((total_res, 128), F32)] * (depth // 128)
+        in_tile = 128 // width
+        for h in range(heads):
+            one = scores[:, h * total_res : (h + 1) * total_res] + extra[h]
+            one = jnp.where(keep, one, -1000000000.0)
+            one = jnp.exp(one - jnp.max(one, axis=-1, keepdims=True))
+            totals[h // in_tile] = jnp.where(
+                head_of == h % in_tile, jnp.sum(one, axis=-1, keepdims=True), totals[h // in_tile]
+            )
+            probs.append(one.astype(BF16))
+        attended = dot(jnp.concatenate(probs, axis=1), value_stack)
+        attended = attended / jnp.concatenate(totals, axis=1)
+        gate = g_ref[:, s].reshape(total_res, depth)
+        gated = (gate * attended).astype(BF16)
+        x = hx[:, s].reshape(total_res, depth).astype(F32)
+        result = (x + dot(gated, wo_ref[...])).astype(BF16)
+        return result.reshape(cols, residues, depth)
+
+    def attend_group(group, carry):
+        first = group * at_once
+        results = [attend(first + n) for n in range(at_once)]
+        for n in range(at_once):
+            hout[:, first + n] = results[n]
+        for step in range(1, cols):
+            peer = lax.rem(col + step, cols)
+            pltpu.make_async_remote_copy(
+                src_ref=hout.at[peer, pl.ds(first, at_once)],
+                dst_ref=msa_out_ref.at[pl.ds(col * seqs + first, at_once)],
+                send_sem=o_send_sem,
+                recv_sem=o_recv_sem,
+                device_id=(row, peer),
+                device_id_type=MESH,
+            ).start()
+        msa_out_ref[pl.ds(col * seqs + first, at_once)] = hout[col, pl.ds(first, at_once)]
+        return carry
+
+    with jax.named_scope("row_attention"):
+        lax.fori_loop(0, seqs // at_once // 2, attend_group, 0)
+
+    wait_for(recv, count - 1, e_recv_sem)
     with jax.named_scope("edge_matrices"):
         to_matrices(0, edge_pieces)
-
-    def matrix(part, q):
-        return zed[part].reshape(2 * rows, 8, 8, lanes)[:, q].reshape(total_res, lanes)
-
     with jax.named_scope("triangle_product"):
         for ch in range(mine):
             left = matrix(0, ch).T.astype(BF16)
@@ -319,61 +379,8 @@
     lax.fori_loop(1, count, push_product, 0)
     precv[pl.ds(me, 1)] = psend[pl.ds(me, 1)]
 
-    wait_for(brecv, (cols - 1) * rows, c_recv_sem)
-    with jax.named_scope("attention_bias"):
-        to_matrices(1, bias_pieces)
-        identity = jnp.broadcast_to(identity_ref[...].astype(F32), (total_res, total_res))
-        cross = (identity.T != identity).astype(F32)
-        for h in range(heads):
-            extra[h] = matrix(1, h) + offset_ref[h] * cross
-
-    keep = keep_ref[...] > 0
-    head_of = lane_blocks((total_res, depth), width)
-    in_head = [(lane_blocks((1, depth), width) == h).astype(F32).astype(BF16) for h in range(heads)]
-    at_once = 2 if seqs % 2 == 0 else 1
-
-    def attend(s):
-        queries = q_ref[:, s].reshape(total_res, depth)
-        keys = k_ref[:, s].reshape(total_res, depth)
-        values = v_ref[:, s].reshape(total_res, depth)
-        key_stack = jnp.concatenate([keys * in_head[h] for h in range(heads)], axis=0)
-        value_stack = jnp.concatenate([values * in_head[h] for h in range(heads)], axis=0)
-        scores = dot(queries, key_stack, ((1,), (1,)))
-        probs = []
-        total = jnp.ones((total_res, depth), F32)
-        for h in range(heads):
-            one = scores[:, h * total_res : (h + 1) * total_res] + extra[h]
-            one = jnp.where(keep, one, -1000000000.0)
-            one = jnp.exp(one - jnp.max(one, axis=-1, keepdims=True))
-            total = jnp.where(head_of == h, jnp.sum(one, axis=-1, keepdims=True), total)
-            probs.append(one.astype(BF16))
-        attended = dot(jnp.concatenate(probs, axis=1), value_stack) / total
-        gate = g_ref[:, s].reshape(total_res, depth)
-        gated = (gate * attended).astype(BF16)
-        x = hx[:, s].reshape(total_res, depth).astype(F32)
-        result = (x + dot(gated, wo_ref[...])).astype(BF16)
-        return result.reshape(cols, residues, depth)
-
-    def attend_group(group, carry):
-        first = group * at_once
-        results = [attend(first + n) for n in range(at_once)]
-        for n in range(at_once):
-            hout[:, first + n] = results[n]
-        for step in range(1, cols):
-            peer = lax.rem(col + step, cols)
-            pltpu.make_async_remote_copy(
-                src_ref=hout.at[peer, pl.ds(first, at_once)],
-                dst_ref=msa_out_ref.at[pl.ds(col * seqs + first, at_once)],
-                send_sem=o_send_sem,
-                recv_sem=o_recv_sem,
-                device_id=(row, peer),
-                device_id_type=MESH,
-            ).start()
-        msa_out_ref[pl.ds(col * seqs + first, at_once)] = hout[col, pl.ds(first, at_once)]
-        return carry
-
     with jax.named_scope("row_attention"):
-        lax.fori_loop(0, seqs // at_once, attend_group, 0)
+        lax.fori_loop(seqs // at_once // 2, seqs // at_once, attend_group, 0)
 
     wait_for(precv, count - 1, p_recv_sem)
     loads[3].wait()

time: 34.8 us -> 36.5 us (1.049)
  Pallas kernels: 31.4 us -> 33.1 us
    pallas_call x1, Pallas kernels: 31.4 us -> 33.1 us  [local_fused(): pl.pallas_call(functools.partial(fused, (rows, cols, heads, cz)), out_sha...]
where the time goes in v3:
time: 36.5 us; the launch traced here: 36.3 us
  Pallas kernels  33.1 us (91%)
  local copies, waits for them, and re-layouts  2.56 us (7%)
  between operations  0.65 us (2%)
    pallas_call x1, Pallas kernels, local_fused(): pl.pallas_call(functools.partial(fused, (rows, cols, heads, cz)), out_sha...  33.1 us
    unnamed x4, local copies, waits for them, and re-layouts  2.56 us

profile of v3, /device:TPU:0, one launch (start us, length us, event | category | flops | bytes accessed | tf_op | source)
XLA Modules:
  0.0 36.3 jit_solution(17903807282895044354)
XLA Ops:
  0.6 33.1 %shard_map.149 = (bf16[32,32,256]{2,1,0:T(8,128)(2,1)}, bf16[16,32,128]{2,1,0:T(8,128)(2,1)}) custom-call(bf16[32,32,256]{2,1,0:T(8,128)(2,1)} %x_ref.1, bf16[16,32,128]{2,1,0:T(8,128)(2,1)} %pair_hbm.1, s32[128]{0:T(128)} %flags_smem.1, s32[1,128]{1,0:T(1,128)} %bitcast.4, s32[1,128]{1,0:T(1,128)} %bitcast.5, f32[8]{0:T(128)} %offset_ref.1, ...), custom_call_target="tpu_custom_call" | custom-call | tf_op jit(solution)/shard_map/pallas_call | solution.py:456
  33.7 0.0 copy-start
  33.7 1.9 %copy.18 = bf16[32,32,256]{2,1,0:T(8,128)(2,1)} copy(bf16[32,32,256]{2,1,0:T(8,128)(2,1)} %get-tuple-element.4) | data formatting | bytes 1048576
  35.6 0.0 copy-done
  35.6 0.7 %copy.19 = bf16[16,32,128]{2,1,0:T(8,128)(2,1)} copy(bf16[16,32,128]{2,1,0:T(8,128)(2,1)S(1)} %copy-done) | data formatting | bytes 262144
Async XLA Ops:
  33.7 1.9 %copy-start = (bf16[16,32,128]{2,1,0:T(8,128)(2,1)S(1)}, bf16[16,32,128]{2,1,0:T(8,128)(2,1)}, u32[]{:S(2)}) copy-start(bf16[16,32,128]{2,1,0:T(8,128)(2,1)} %get-tuple-element.5) | copy-start | bytes 393220

commit v4 on v2

--- a/solution.py
+++ b/solution.py
@@ -65,6 +65,8 @@
     k_ref,
     v_ref,
     g_ref,
+    key_blocks,
+    value_blocks,
     pair_ref,
     wq_ref,
     wg_ref,
@@ -88,6 +90,7 @@
     r_recv_sem,
     c_send_sem,
     c_recv_sem,
+    keep_sem,
 ):
     rows, cols, heads, channels = dims
     count = rows * cols
@@ -101,6 +104,7 @@
     pair_rows, pair_cols, cz = pair_ref.shape
     positions = pair_rows * pair_cols
     half = positions // 2
+    at_once = key_blocks.shape[0]
     both = 2 * cz
 
     def other(step):
@@ -135,6 +139,8 @@
     own.start()
     lax.fori_loop(1, count, greet, 0)
 
+    key_blocks[...] = jnp.zeros_like(key_blocks)
+    value_blocks[...] = jnp.zeros_like(value_blocks)
     with jax.named_scope("weights_by_owner"):
         to = lax.broadcasted_iota(jnp.int32, (both, both), 0)
         source = lax.broadcasted_iota(jnp.int32, (both, both), 1)
@@ -154,7 +160,19 @@
             for n in range(2)
         ]
 
-    with jax.named_scope("pair_edges_and_bias"):
+    pl.semaphore_wait(barrier, count - 1)
+    for step in range(1, cols):
+        peer = lax.rem(col + step, cols)
+        pltpu.make_async_remote_copy(
+            src_ref=x_ref.at[pl.ds(peer * seqs, seqs)],
+            dst_ref=hx.at[col],
+            send_sem=x_send_sem,
+            recv_sem=x_recv_sem,
+            device_id=(row, peer),
+            device_id_type=MESH,
+        ).start()
+
+    with jax.named_scope("pair_bias"):
         loads[0].wait()
         pair = pair_ref[...].astype(F32).reshape(positions, cz)
         pn = normalize(pair, -1).astype(BF16)
@@ -162,6 +180,18 @@
         bias = dot(bias_w_ref[...], pn, ((1,), (1,)))
         bias = jnp.concatenate([bias[:, :half], bias[:, half:]], axis=0).astype(BF16)
         brecv[pl.ds(col * rows + row, 1)] = bias[None]
+
+    for step in range(1, rows):
+        pltpu.make_async_remote_copy(
+            src_ref=brecv.at[col * rows + row],
+            dst_ref=brecv.at[col * rows + row],
+            send_sem=r_send_sem,
+            recv_sem=r_recv_sem,
+            device_id=(lax.rem(row + step, rows), col),
+            device_id_type=MESH,
+        ).start()
+
+    with jax.named_scope("pair_edges"):
         k_of = lane_blocks((1, positions), pair_cols)
         mask = jnp.zeros((1, positions), F32)
         for k in range(pair_rows):
@@ -173,18 +203,6 @@
         )
         edge = edge.reshape(count, 2 * mine, positions)
         send[...] = jnp.concatenate([edge[:, :, :half], edge[:, :, half:]], axis=1).astype(BF16)
-
-    pl.semaphore_wait(barrier, count - 1)
-
-    for step in range(1, rows):
-        pltpu.make_async_remote_copy(
-            src_ref=brecv.at[col * rows + row],
-            dst_ref=brecv.at[col * rows + row],
-            send_sem=r_send_sem,
-            recv_sem=r_recv_sem,
-            device_id=(lax.rem(row + step, rows), col),
-            device_id_type=MESH,
-        ).start()
 
     def push(step, carry):
         to_row, to_col = other(step)
@@ -200,16 +218,6 @@
         return carry
 
     lax.fori_loop(1, count, push, 0)
-    for step in range(1, cols):
-        peer = lax.rem(col + step, cols)
-        pltpu.make_async_remote_copy(
-            src_ref=x_ref.at[pl.ds(peer * seqs, seqs)],
-            dst_ref=hx.at[col],
-            send_sem=x_send_sem,
-            recv_sem=x_recv_sem,
-            device_id=(row, peer),
-            device_id_type=MESH,
-        ).start()
     recv[pl.ds(me, 1)] = send[pl.ds(me, 1)]
 
     def wait_for(ref, number, sem):
@@ -232,18 +240,14 @@
     for load in loads[5:]:
         load.wait()
     with jax.named_scope("projections"):
-        for c in range(cols):
-            shape = (seqs, residues, depth)
-            x = hx[c].reshape(seqs * residues, depth).astype(F32)
-            xn = normalize(x, -1).astype(BF16)
-            queries = dot(xn, wq_ref[...]) * width ** (-0.5)
-            q_ref[c] = queries.astype(BF16).reshape(shape)
-            kv = dot(xn, wkv_ref[...]).astype(BF16)
-            k_ref[c] = kv[:, :depth].reshape(shape)
-            v_ref[c] = kv[:, depth:].reshape(shape)
-            g_ref[c] = jax.nn.sigmoid(dot(xn, wg_ref[...])).reshape(shape)
-
-    wait_for(recv, count - 1, e_recv_sem)
+        key_w = wkv_ref[:, :depth].astype(F32).T.astype(BF16)
+        for g in range(seqs // at_once):
+            x = [hx[:, g * at_once + n].reshape(total_res, depth) for n in range(at_once)]
+            xn = normalize(jnp.concatenate(x, axis=0).astype(F32), -1).astype(BF16)
+            q_ref[g] = (dot(xn, wq_ref[...]) * width ** (-0.5)).astype(BF16)
+            k_ref[g] = dot(key_w, xn, ((1,), (1,))).astype(BF16)
+            v_ref[g] = dot(xn, wkv_ref[:, depth:]).astype(BF16)
+            g_ref[g] = jax.nn.sigmoid(dot(xn, wg_ref[...]))
 
     block = pair_cols
     lanes = total_res
@@ -271,12 +275,12 @@
         taken = taken.astype(F32).reshape(cols, 16 * rows, lanes)
         return [taken[c] for c in range(cols)]
 
+    def matrix(part, q):
+        return zed[part].reshape(2 * rows, 8, 8, lanes)[:, q].reshape(total_res, lanes)
+
+    wait_for(recv, count - 1, e_recv_sem)
     with jax.named_scope("edge_matrices"):
         to_matrices(0, edge_pieces)
-
-    def matrix(part, q):
-        return zed[part].reshape(2 * rows, 8, 8, lanes)[:, q].reshape(total_res, lanes)
-
     with jax.named_scope("triangle_product"):
         for ch in range(mine):
             left = matrix(0, ch).T.astype(BF16)
@@ -328,35 +332,40 @@
             extra[h] = matrix(1, h) + offset_ref[h] * cross
 
     keep = keep_ref[...] > 0
-    head_of = lane_blocks((total_res, depth), width)
-    in_head = [(lane_blocks((1, depth), width) == h).astype(F32).astype(BF16) for h in range(heads)]
-    at_once = 2 if seqs % 2 == 0 else 1
-
-    def attend(s):
-        queries = q_ref[:, s].reshape(total_res, depth)
-        keys = k_ref[:, s].reshape(total_res, depth)
-        values = v_ref[:, s].reshape(total_res, depth)
-        key_stack = jnp.concatenate([keys * in_head[h] for h in range(heads)], axis=0)
-        value_stack = jnp.concatenate([values * in_head[h] for h in range(heads)], axis=0)
-        scores = dot(queries, key_stack, ((1,), (1,)))
+    head_of = lane_blocks((total_res, 128), width)
+    in_tile = 128 // width
+    in_head = [(lane_blocks((1, 128), width) == h).astype(F32).astype(BF16) for h in range(in_tile)]
+
+    def attend(group, n):
+        here = slice(n * total_res, (n + 1) * total_res)
+        for h in range(heads):
+            down = slice(h * width, (h + 1) * width)
+            across = slice(h * total_res, (h + 1) * total_res)
+            tile = slice(h // in_tile * 128, (h // in_tile + 1) * 128)
+            key_blocks[n, down, across] = k_ref[group, down, here]
+            value_blocks[n, across, tile] = v_ref[group, here, tile] * in_head[h % in_tile]
+        scores = dot(q_ref[group, here], key_blocks[n])
         probs = []
-        total = jnp.ones((total_res, depth), F32)
+        totals = [jnp.ones((total_res, 128), F32)] * (depth // 128)
         for h in range(heads):
             one = scores[:, h * total_res : (h + 1) * total_res] + extra[h]
             one = jnp.where(keep, one, -1000000000.0)
             one = jnp.exp(one - jnp.max(one, axis=-1, keepdims=True))
-            total = jnp.where(head_of == h, jnp.sum(one, axis=-1, keepdims=True), total)
+            totals[h // in_tile] = jnp.where(
+                head_of == h % in_tile, jnp.sum(one, axis=-1, keepdims=True), totals[h // in_tile]
+            )
             probs.append(one.astype(BF16))
-        attended = dot(jnp.concatenate(probs, axis=1), value_stack) / total
-        gate = g_ref[:, s].reshape(total_res, depth)
+        attended = dot(jnp.concatenate(probs, axis=1), value_blocks[n])
+        attended = attended / jnp.concatenate(totals, axis=1)
+        gate = g_ref[group, here]
         gated = (gate * attended).astype(BF16)
-        x = hx[:, s].reshape(total_res, depth).astype(F32)
+        x = hx[:, group * at_once + n].reshape(total_res, depth).astype(F32)
         result = (x + dot(gated, wo_ref[...])).astype(BF16)
         return result.reshape(cols, residues, depth)
 
     def attend_group(group, carry):
         first = group * at_once
-        results = [attend(first + n) for n in range(at_once)]
+        results = [attend(group, n) for n in range(at_once)]
         for n in range(at_once):
             hout[:, first + n] = results[n]
         for step in range(1, cols):
@@ -369,7 +378,11 @@
                 device_id=(row, peer),
                 device_id_type=MESH,
             ).start()
-        msa_out_ref[pl.ds(col * seqs + first, at_once)] = hout[col, pl.ds(first, at_once)]
+        pltpu.make_async_copy(
+            hout.at[col, pl.ds(first, at_once)],
+            msa_out_ref.at[pl.ds(col * seqs + first, at_once)],
+            keep_sem,
+        ).start()
         return carry
 
     with jax.named_scope("row_attention"):
@@ -413,6 +426,21 @@
     wait_for(brecv, (cols - 1) * rows, c_send_sem)
     wait_for(hout, cols - 1, o_send_sem)
     wait_for(hout, cols - 1, o_recv_sem)
+    wait_for(hout, 1, keep_sem)
+
+
+def deliver(msa_ref, pair_ref, msa_out_ref, pair_out_ref, sem):
+    part = msa_ref.shape[0] // 4
+    copies = [
+        pltpu.make_async_copy(
+            msa_ref.at[pl.ds(n * part, part)], msa_out_ref.at[pl.ds(n * part, part)], sem.at[n]
+        )
+        for n in range(4)
+    ] + [pltpu.make_async_copy(pair_ref, pair_out_ref, sem.at[4])]
+    for copy in copies:
+        copy.start()
+    for copy in copies:
+        copy.wait()
 
 
 def local_fused(
@@ -446,14 +474,14 @@
     hbm = pl.BlockSpec(memory_space=pltpu.HBM)
     dma = pltpu.SemaphoreType.DMA
     msa_block = (cols, seqs, residues, depth)
-    return pl.pallas_call(
+    results = pl.pallas_call(
         functools.partial(fused, (rows, cols, heads, cz)),
         out_shape=(
             jax.ShapeDtypeStruct(homolog_tensor.shape, BF16),
             jax.ShapeDtypeStruct(pairwise_tensor.shape, BF16),
         ),
         in_specs=[hbm, hbm, smem, vmem, vmem, smem] + [hbm] * 4 + [vmem] + [hbm] * 4,
-        out_specs=(vmem, vmem),
+        out_specs=(hbm, vmem),
         scratch_shapes=[
             pltpu.VMEM(msa_block, BF16),
             pltpu.VMEM(msa_block, BF16),
@@ -466,10 +494,12 @@
             pltpu.VMEM((2 * rows, mine, 8, total_res), F32),
             pltpu.VMEM((heads, total_res, total_res), F32),
             pltpu.VMEM((pair_rows * pair_cols, cz), BF16),
-            pltpu.VMEM(msa_block, BF16),
-            pltpu.VMEM(msa_block, BF16),
-            pltpu.VMEM(msa_block, BF16),
-            pltpu.VMEM(msa_block, F32),
+            pltpu.VMEM((seqs // 2, 2 * total_res, depth), BF16),
+            pltpu.VMEM((seqs // 2, depth, 2 * total_res), BF16),
+            pltpu.VMEM((seqs // 2, 2 * total_res, depth), BF16),
+            pltpu.VMEM((seqs // 2, 2 * total_res, depth), F32),
+            pltpu.VMEM((2, depth, heads * total_res), BF16),
+            pltpu.VMEM((2, heads * total_res, depth), BF16),
             pltpu.VMEM((pair_rows, pair_cols, cz), BF16),
             pltpu.VMEM(asking_weights.shape, BF16),
             pltpu.VMEM(attend_sigmoid_weights.shape, BF16),
@@ -481,7 +511,7 @@
             pltpu.VMEM(trimult_final_weights.shape, BF16),
             dma((9,)),
         ]
-        + [dma] * 13,
+        + [dma] * 14,
         compiler_params=pltpu.CompilerParams(
             collective_id=0, has_side_effects=True, vmem_limit_bytes=62 * 2**20
         ),
@@ -502,6 +532,14 @@
         trimult_sigmoid_weights,
         trimult_final_weights,
     )
+    return pl.pallas_call(
+        deliver,
+        out_shape=tuple(jax.ShapeDtypeStruct(r.shape, r.dtype) for r in results),
+        in_specs=[hbm, hbm],
+        out_specs=(hbm, hbm),
+        scratch_shapes=[dma((5,))],
+        compiler_params=pltpu.CompilerParams(vmem_limit_bytes=62 * 2**20),
+    )(*results)
 
 
 def from_root(array, axis, root):
@@ -669,7 +707,7 @@
             and pair_cols == residues == 32
             and pair_rows == 16
             and heads == 8
-            and homologs % cols == 0
+            and homologs % (2 * cols) == 0
             and blocks[4].shape[1] == depth
             and depth % 128 == 0
         )

time: 34.8 us -> 53.3 us (1.53)
  Pallas kernels: 31.4 us -> 52.5 us
  local copies, waits for them, and re-layouts: 2.56 us -> 0 us
    pallas_call x0 -> x1, Pallas kernels: none -> 21 us  [local_fused(): pl.pallas_call(deliver, out_shape=tuple((jax.ShapeDtypeStruct(r.shape, r....]
    unnamed x4 -> x0, local copies, waits for them, and re-layouts: 2.56 us -> none
where the time goes in v4:
time: 53.3 us; the launch traced here: 53.2 us
  Pallas kernels  52.5 us (98%)
  between operations  0.64 us (1%)
    pallas_call x1, Pallas kernels, local_fused(): pl.pallas_call(functools.partial(fused, (rows, cols, heads, cz)), out_sha...  31.5 us
    pallas_call x1, Pallas kernels, local_fused(): pl.pallas_call(deliver, out_shape=tuple((jax.ShapeDtypeStruct(r.shape, r....  21 us

profile of v4, /device:TPU:0, one launch (start us, length us, event | category | flops | bytes accessed | tf_op | source)
XLA Modules:
  0.0 53.2 jit_solution(6462926872221880234)
XLA Ops:
  0.6 31.5 %shard_map.149 = (bf16[32,32,256]{2,1,0:T(8,128)(2,1)}, bf16[16,32,128]{2,1,0:T(8,128)(2,1)}) custom-call(bf16[32,32,256]{2,1,0:T(8,128)(2,1)} %x_ref.1, bf16[16,32,128]{2,1,0:T(8,128)(2,1)} %pair_hbm.1, s32[128]{0:T(128)} %flags_smem.1, s32[1,128]{1,0:T(1,128)} %bitcast.4, s32[1,128]{1,0:T(1,128)} %bitcast.5, f32[8]{0:T(128)} %offset_ref.1, ...), custom_call_target="tpu_custom_call" | custom-call | tf_op jit(solution)/shard_map/pallas_call | solution.py:477
  32.2 21.0 %shard_map.150 = (bf16[32,32,256]{2,1,0:T(8,128)(2,1)}, bf16[16,32,128]{2,1,0:T(8,128)(2,1)}) custom-call(bf16[32,32,256]{2,1,0:T(8,128)(2,1)} %get-tuple-element.4.msa_ref, bf16[16,32,128]{2,1,0:T(8,128)(2,1)} %get-tuple-element.5.pair_ref), custom_call_target="tpu_custom_call" | custom-call | tf_op jit(solution)/shard_map/pallas_call | solution.py:535

commit v5 on v4

--- a/solution.py
+++ b/solution.py
@@ -53,9 +53,11 @@
     hx,
     hout,
     send,
+    landed,
     recv,
     brecv,
     psend,
+    planded,
     precv,
     zed,
     zprod,
@@ -91,6 +93,10 @@
     c_send_sem,
     c_recv_sem,
     keep_sem,
+    f_send_sem,
+    f_recv_sem,
+    s_send_sem,
+    s_recv_sem,
 ):
     rows, cols, heads, channels = dims
     count = rows * cols
@@ -107,15 +113,9 @@
     at_once = key_blocks.shape[0]
     both = 2 * cz
 
-    def other(step):
-        peer = lax.rem(me + step, count)
-        return peer // cols, lax.rem(peer, cols)
-
     barrier = pltpu.get_barrier_semaphore()
-
-    def greet(step, carry):
-        pl.semaphore_signal(barrier, inc=1, device_id=other(step), device_id_type=MESH)
-        return carry
+    row_peers = [(lax.rem(row + step, rows), col) for step in range(1, rows)]
+    col_peers = [(row, lax.rem(col + step, cols)) for step in range(1, cols)]
 
     loads = [
         pltpu.make_async_copy(source, target, in_sem.at[n])
@@ -137,7 +137,8 @@
         load.start()
     own = pltpu.make_async_copy(x_ref.at[pl.ds(col * seqs, seqs)], hx.at[col], own_sem)
     own.start()
-    lax.fori_loop(1, count, greet, 0)
+    for peer in row_peers + col_peers:
+        pl.semaphore_signal(barrier, inc=1, device_id=peer, device_id_type=MESH)
 
     key_blocks[...] = jnp.zeros_like(key_blocks)
     value_blocks[...] = jnp.zeros_like(value_blocks)
@@ -160,7 +161,7 @@
             for n in range(2)
         ]
 
-    pl.semaphore_wait(barrier, count - 1)
+    pl.semaphore_wait(barrier, rows + cols - 2)
     for step in range(1, cols):
         peer = lax.rem(col + step, cols)
         pltpu.make_async_remote_copy(
@@ -202,23 +203,34 @@
             * dot(edge_w[1], pn, ((1,), (1,)))
         )
         edge = edge.reshape(count, 2 * mine, positions)
-        send[...] = jnp.concatenate([edge[:, :, :half], edge[:, :, half:]], axis=1).astype(BF16)
-
-    def push(step, carry):
-        to_row, to_col = other(step)
-        slot = to_row * cols + to_col
-        pltpu.make_async_remote_copy(
-            src_ref=send.at[slot],
-            dst_ref=recv.at[me],
-            send_sem=e_send_sem,
-            recv_sem=e_recv_sem,
-            device_id=(to_row, to_col),
-            device_id_type=MESH,
-        ).start()
-        return carry
-
-    lax.fori_loop(1, count, push, 0)
-    recv[pl.ds(me, 1)] = send[pl.ds(me, 1)]
+        edge = jnp.concatenate([edge[:, :, :half], edge[:, :, half:]], axis=1)
+        send[...] = edge.astype(BF16).reshape(send.shape)
+
+    def along_row(source, landing, send_sem, recv_sem):
+        for peer in row_peers:
+            pltpu.make_async_remote_copy(
+                src_ref=source.at[peer[0]],
+                dst_ref=landing.at[row],
+                send_sem=send_sem,
+                recv_sem=recv_sem,
+                device_id=peer,
+                device_id_type=MESH,
+            ).start()
+        landing[pl.ds(row, 1)] = source[pl.ds(row, 1)]
+
+    def along_col(landing, target, send_sem, recv_sem):
+        for peer in col_peers:
+            pltpu.make_async_remote_copy(
+                src_ref=landing.at[:, peer[1]],
+                dst_ref=target.at[col],
+                send_sem=send_sem,
+                recv_sem=recv_sem,
+                device_id=peer,
+                device_id_type=MESH,
+            ).start()
+        target[pl.ds(col, 1)] = landing[:, pl.ds(col, 1)].reshape((1,) + target.shape[1:])
+
+    along_row(send, landed, e_send_sem, e_recv_sem)
 
     def wait_for(ref, number, sem):
         part = ref.at[pl.ds(0, number)]
@@ -235,6 +247,8 @@
             device_id_type=MESH,
         ).start()
 
+    wait_for(landed, rows - 1, e_recv_sem)
+    along_col(landed, recv, f_send_sem, f_recv_sem)
     own.wait()
     wait_for(hx, cols - 1, x_recv_sem)
     for load in loads[5:]:
@@ -266,9 +280,8 @@
                 zed[part, pl.ds(tile * per_tile + k, 16 * rows, stride=8), :] = merged
 
     def edge_pieces(tile):
-        taken = recv[:, :, tile * lanes : (tile + 1) * lanes]
-        taken = taken.astype(F32).reshape(rows, cols, 16, lanes)
-        return [taken[:, c].reshape(16 * rows, lanes) for c in range(cols)]
+        taken = recv[:, :, :, tile * lanes : (tile + 1) * lanes].astype(F32)
+        return [taken[c].reshape(16 * rows, lanes) for c in range(cols)]
 
     def bias_pieces(tile):
         taken = brecv[:, :, tile * lanes : (tile + 1) * lanes]
@@ -278,7 +291,7 @@
     def matrix(part, q):
         return zed[part].reshape(2 * rows, 8, 8, lanes)[:, q].reshape(total_res, lanes)
 
-    wait_for(recv, count - 1, e_recv_sem)
+    wait_for(recv, cols - 1, f_recv_sem)
     with jax.named_scope("edge_matrices"):
         to_matrices(0, edge_pieces)
     with jax.named_scope("triangle_product"):
@@ -303,25 +316,11 @@
                         where_small == k, shift_lanes(taken[k], (k - c) * block), merged
                     )
                 merged_all.append(merged.reshape(rows, 2 * mine, lanes))
-            psend[:, :, tile * lanes : (tile + 1) * lanes] = jnp.stack(
+            psend[:, :, :, tile * lanes : (tile + 1) * lanes] = jnp.stack(
                 merged_all, axis=1
-            ).reshape(count, 2 * mine, lanes)
-
-    def push_product(step, carry):
-        to_row, to_col = other(step)
-        slot = to_row * cols + to_col
-        pltpu.make_async_remote_copy(
-            src_ref=psend.at[slot],
-            dst_ref=precv.at[me],
-            send_sem=p_send_sem,
-            recv_sem=p_recv_sem,
-            device_id=(to_row, to_col),
-            device_id_type=MESH,
-        ).start()
-        return carry
-
-    lax.fori_loop(1, count, push_product, 0)
-    precv[pl.ds(me, 1)] = psend[pl.ds(me, 1)]
+            )
+
+    along_row(psend, planded, p_send_sem, p_recv_sem)
 
     wait_for(brecv, (cols - 1) * rows, c_recv_sem)
     with jax.named_scope("attention_bias"):
@@ -386,13 +385,18 @@
         return carry
 
     with jax.named_scope("row_attention"):
-        lax.fori_loop(0, seqs // at_once, attend_group, 0)
-
-    wait_for(precv, count - 1, p_recv_sem)
+        lax.fori_loop(0, seqs // at_once // 2, attend_group, 0)
+
+    wait_for(planded, rows - 1, p_recv_sem)
+    along_col(planded, precv, s_send_sem, s_recv_sem)
+    with jax.named_scope("row_attention"):
+        lax.fori_loop(seqs // at_once // 2, seqs // at_once, attend_group, 0)
+
+    wait_for(precv, cols - 1, s_recv_sem)
     loads[3].wait()
     loads[4].wait()
     with jax.named_scope("pair_update"):
-        product = precv[...]
+        product = precv[...].reshape(count, 2 * mine, half)
         in_half = lax.broadcasted_iota(jnp.int32, (8, half), 0) < mine
 
         def spread_halves(partial):
@@ -405,7 +409,8 @@
         norm = (center * lax.rsqrt(spread + 1e-05)[None]).reshape(count * 8, half)
         to = lax.broadcasted_iota(jnp.int32, (2 * channels, channels), 0)
         source = lax.broadcasted_iota(jnp.int32, (2 * channels, channels), 1)
-        wanted = to // (2 * mine) * mine + to % mine
+        slot = to // (2 * mine)
+        wanted = (slot % rows * cols + slot // rows) * mine + to % mine
         final_w = dot((source == wanted).astype(BF16), tri_out_w_ref[...])
         low_rows = to % (2 * mine) < mine
         final_w = jnp.concatenate(
@@ -420,8 +425,10 @@
         )
 
     wait_for(hx, cols - 1, x_send_sem)
-    wait_for(send, count - 1, e_send_sem)
-    wait_for(psend, count - 1, p_send_sem)
+    wait_for(send, rows - 1, e_send_sem)
+    wait_for(psend, rows - 1, p_send_sem)
+    wait_for(recv, cols - 1, f_send_sem)
+    wait_for(precv, cols - 1, s_send_sem)
     wait_for(brecv, rows - 1, r_send_sem)
     wait_for(brecv, (cols - 1) * rows, c_send_sem)
     wait_for(hout, cols - 1, o_send_sem)
@@ -429,18 +436,25 @@
     wait_for(hout, 1, keep_sem)
 
 
-def deliver(msa_ref, pair_ref, msa_out_ref, pair_out_ref, sem):
+def deliver(msa_ref, pair_ref, msa_out_ref, pair_out_ref, msa_vmem, pair_vmem, in_sem, out_sem):
     part = msa_ref.shape[0] // 4
-    copies = [
-        pltpu.make_async_copy(
-            msa_ref.at[pl.ds(n * part, part)], msa_out_ref.at[pl.ds(n * part, part)], sem.at[n]
+    moves = [
+        (
+            msa_ref.at[pl.ds(n * part, part)],
+            msa_vmem.at[pl.ds(n * part, part)],
+            msa_out_ref.at[pl.ds(n * part, part)],
         )
         for n in range(4)
-    ] + [pltpu.make_async_copy(pair_ref, pair_out_ref, sem.at[4])]
-    for copy in copies:
-        copy.start()
-    for copy in copies:
-        copy.wait()
+    ] + [(pair_ref, pair_vmem, pair_out_ref)]
+    loads = [pltpu.make_async_copy(a, b, in_sem.at[n]) for n, (a, b, _) in enumerate(moves)]
+    stores = [pltpu.make_async_copy(b, c, out_sem.at[n]) for n, (_, b, c) in enumerate(moves)]
+    for load in loads:
+        load.start()
+    for load, store in zip(loads, stores):
+        load.wait()
+        store.start()
+    for store in stores:
+        store.wait()
 
 
 def local_fused(
@@ -485,11 +499,13 @@
         scratch_shapes=[
             pltpu.VMEM(msa_block, BF16),
             pltpu.VMEM(msa_block, BF16),
+            pltpu.VMEM((rows, cols, 16, half), BF16),
+            pltpu.VMEM((rows, cols, 16, half), BF16),
+            pltpu.VMEM((cols, rows, 16, half), BF16),
             pltpu.VMEM((count, 16, half), BF16),
-            pltpu.VMEM((count, 16, half), BF16),
-            pltpu.VMEM((count, 16, half), BF16),
-            pltpu.VMEM((count, 2 * mine, half), F32),
-            pltpu.VMEM((count, 2 * mine, half), F32),
+            pltpu.VMEM((rows, cols, 2 * mine, half), F32),
+            pltpu.VMEM((rows, cols, 2 * mine, half), F32),
+            pltpu.VMEM((cols, rows, 2 * mine, half), F32),
             pltpu.VMEM((2, 8 * total_res, total_res), F32),
             pltpu.VMEM((2 * rows, mine, 8, total_res), F32),
             pltpu.VMEM((heads, total_res, total_res), F32),
@@ -511,7 +527,7 @@
             pltpu.VMEM(trimult_final_weights.shape, BF16),
             dma((9,)),
         ]
-        + [dma] * 14,
+        + [dma] * 18,
         compiler_params=pltpu.CompilerParams(
             collective_id=0, has_side_effects=True, vmem_limit_bytes=62 * 2**20
         ),
@@ -537,7 +553,7 @@
         out_shape=tuple(jax.ShapeDtypeStruct(r.shape, r.dtype) for r in results),
         in_specs=[hbm, hbm],
         out_specs=(hbm, hbm),
-        scratch_shapes=[dma((5,))],
+        scratch_shapes=[pltpu.VMEM(r.shape, r.dtype) for r in results] + [dma((5,)), dma((5,))],
         compiler_params=pltpu.CompilerParams(vmem_limit_bytes=62 * 2**20),
     )(*results)
 

time: 53.3 us -> 36.9 us (0.69)
  Pallas kernels: 52.5 us -> 36 us
    pallas_call x1, Pallas kernels: 21 us -> 1.91 us  [local_fused(): pl.pallas_call(deliver, out_shape=tuple((jax.ShapeDtypeStruct(r.shape, r....]
    pallas_call x1, Pallas kernels: 31.5 us -> 34.1 us  [local_fused(): pl.pallas_call(functools.partial(fused, (rows, cols, heads, cz)), out_sha...]
where the time goes in v5:
time: 36.9 us; the launch traced here: 36.7 us
  Pallas kernels  36 us (98%)
  between operations  0.64 us (2%)
    pallas_call x1, Pallas kernels, local_fused(): pl.pallas_call(functools.partial(fused, (rows, cols, heads, cz)), out_sha...  34.1 us
    pallas_call x1, Pallas kernels, local_fused(): pl.pallas_call(deliver, out_shape=tuple((jax.ShapeDtypeStruct(r.shape, r....  1.91 us

profile of v5, /device:TPU:0, one launch (start us, length us, event | category | flops | bytes accessed | tf_op | source)
XLA Modules:
  0.0 36.7 jit_solution(17518252532247388165)
XLA Ops:
  0.6 34.1 %shard_map.149 = (bf16[32,32,256]{2,1,0:T(8,128)(2,1)}, bf16[16,32,128]{2,1,0:T(8,128)(2,1)}) custom-call(bf16[32,32,256]{2,1,0:T(8,128)(2,1)} %x_ref.1, bf16[16,32,128]{2,1,0:T(8,128)(2,1)} %pair_hbm.1, s32[128]{0:T(128)} %flags_smem.1, s32[1,128]{1,0:T(1,128)} %bitcast.4, s32[1,128]{1,0:T(1,128)} %bitcast.5, f32[8]{0:T(128)} %offset_ref.1, ...), custom_call_target="tpu_custom_call" | custom-call | tf_op jit(solution)/shard_map/pallas_call | solution.py:491
  34.8 1.9 %shard_map.150 = (bf16[32,32,256]{2,1,0:T(8,128)(2,1)}, bf16[16,32,128]{2,1,0:T(8,128)(2,1)}) custom-call(bf16[32,32,256]{2,1,0:T(8,128)(2,1)} %get-tuple-element.4.msa_ref, bf16[16,32,128]{2,1,0:T(8,128)(2,1)} %get-tuple-element.5.pair_ref), custom_call_target="tpu_custom_call" | custom-call | tf_op jit(solution)/shard_map/pallas_call | solution.py:551

commit v6 on v4

--- a/solution.py
+++ b/solution.py
@@ -167,7 +167,7 @@
             src_ref=x_ref.at[pl.ds(peer * seqs, seqs)],
             dst_ref=hx.at[col],
             send_sem=x_send_sem,
-            recv_sem=x_recv_sem,
+            recv_sem=x_recv_sem.at[step],
             device_id=(row, peer),
             device_id_type=MESH,
         ).start()
@@ -235,19 +235,24 @@
             device_id_type=MESH,
         ).start()
 
-    own.wait()
-    wait_for(hx, cols - 1, x_recv_sem)
     for load in loads[5:]:
         load.wait()
     with jax.named_scope("projections"):
-        key_w = wkv_ref[:, :depth].astype(F32).T.astype(BF16)
-        for g in range(seqs // at_once):
-            x = [hx[:, g * at_once + n].reshape(total_res, depth) for n in range(at_once)]
-            xn = normalize(jnp.concatenate(x, axis=0).astype(F32), -1).astype(BF16)
-            q_ref[g] = (dot(xn, wq_ref[...]) * width ** (-0.5)).astype(BF16)
-            k_ref[g] = dot(key_w, xn, ((1,), (1,))).astype(BF16)
-            v_ref[g] = dot(xn, wkv_ref[:, depth:]).astype(BF16)
-            g_ref[g] = jax.nn.sigmoid(dot(xn, wg_ref[...]))
+        for step in range(cols):
+            if step == 0:
+                own.wait()
+            else:
+                pltpu.make_async_copy(hx.at[0], hx.at[0], x_recv_sem.at[step]).wait()
+            c = lax.rem(col + cols - step, cols)
+            shape = (1, seqs, residues, depth)
+            x = hx[pl.ds(c, 1)].reshape(seqs * residues, depth).astype(F32)
+            xn = normalize(x, -1).astype(BF16)
+            queries = dot(xn, wq_ref[...]) * width ** (-0.5)
+            q_ref[pl.ds(c, 1)] = queries.astype(BF16).reshape(shape)
+            kv = dot(xn, wkv_ref[...]).astype(BF16)
+            k_ref[pl.ds(c, 1)] = kv[:, :depth].reshape(shape)
+            v_ref[pl.ds(c, 1)] = kv[:, depth:].reshape(shape)
+            g_ref[pl.ds(c, 1)] = jax.nn.sigmoid(dot(xn, wg_ref[...])).reshape(shape)
 
     block = pair_cols
     lanes = total_res
@@ -337,14 +342,16 @@
     in_head = [(lane_blocks((1, 128), width) == h).astype(F32).astype(BF16) for h in range(in_tile)]
 
     def attend(group, n):
-        here = slice(n * total_res, (n + 1) * total_res)
+        s = group * at_once + n
+        keys = k_ref[:, s].reshape(total_res, depth)
+        values = v_ref[:, s].reshape(total_res, depth)
         for h in range(heads):
-            down = slice(h * width, (h + 1) * width)
-            across = slice(h * total_res, (h + 1) * total_res)
+            down = slice(h * total_res, (h + 1) * total_res)
             tile = slice(h // in_tile * 128, (h // in_tile + 1) * 128)
-            key_blocks[n, down, across] = k_ref[group, down, here]
-            value_blocks[n, across, tile] = v_ref[group, here, tile] * in_head[h % in_tile]
-        scores = dot(q_ref[group, here], key_blocks[n])
+            key_blocks[n, down, tile] = keys[:, tile] * in_head[h % in_tile]
+            value_blocks[n, down, tile] = values[:, tile] * in_head[h % in_tile]
+        queries = q_ref[:, s].reshape(total_res, depth)
+        scores = dot(queries, key_blocks[n], ((1,), (1,)))
         probs = []
         totals = [jnp.ones((total_res, 128), F32)] * (depth // 128)
         for h in range(heads):
@@ -357,9 +364,9 @@
             probs.append(one.astype(BF16))
         attended = dot(jnp.concatenate(probs, axis=1), value_blocks[n])
         attended = attended / jnp.concatenate(totals, axis=1)
-        gate = g_ref[group, here]
+        gate = g_ref[:, s].reshape(total_res, depth)
         gated = (gate * attended).astype(BF16)
-        x = hx[:, group * at_once + n].reshape(total_res, depth).astype(F32)
+        x = hx[:, s].reshape(total_res, depth).astype(F32)
         result = (x + dot(gated, wo_ref[...])).astype(BF16)
         return result.reshape(cols, residues, depth)
 
@@ -429,18 +436,25 @@
     wait_for(hout, 1, keep_sem)
 
 
-def deliver(msa_ref, pair_ref, msa_out_ref, pair_out_ref, sem):
+def deliver(msa_ref, pair_ref, msa_out_ref, pair_out_ref, msa_vmem, pair_vmem, in_sem, out_sem):
     part = msa_ref.shape[0] // 4
-    copies = [
-        pltpu.make_async_copy(
-            msa_ref.at[pl.ds(n * part, part)], msa_out_ref.at[pl.ds(n * part, part)], sem.at[n]
+    moves = [
+        (
+            msa_ref.at[pl.ds(n * part, part)],
+            msa_vmem.at[pl.ds(n * part, part)],
+            msa_out_ref.at[pl.ds(n * part, part)],
         )
         for n in range(4)
-    ] + [pltpu.make_async_copy(pair_ref, pair_out_ref, sem.at[4])]
-    for copy in copies:
-        copy.start()
-    for copy in copies:
-        copy.wait()
+    ] + [(pair_ref, pair_vmem, pair_out_ref)]
+    loads = [pltpu.make_async_copy(a, b, in_sem.at[n]) for n, (a, b, _) in enumerate(moves)]
+    stores = [pltpu.make_async_copy(b, c, out_sem.at[n]) for n, (_, b, c) in enumerate(moves)]
+    for load in loads:
+        load.start()
+    for load, store in zip(loads, stores):
+        load.wait()
+        store.start()
+    for store in stores:
+        store.wait()
 
 
 def local_fused(
@@ -494,11 +508,11 @@
             pltpu.VMEM((2 * rows, mine, 8, total_res), F32),
             pltpu.VMEM((heads, total_res, total_res), F32),
             pltpu.VMEM((pair_rows * pair_cols, cz), BF16),
-            pltpu.VMEM((seqs // 2, 2 * total_res, depth), BF16),
-            pltpu.VMEM((seqs // 2, depth, 2 * total_res), BF16),
-            pltpu.VMEM((seqs // 2, 2 * total_res, depth), BF16),
-            pltpu.VMEM((seqs // 2, 2 * total_res, depth), F32),
-            pltpu.VMEM((2, depth, heads * total_res), BF16),
+            pltpu.VMEM(msa_block, BF16),
+            pltpu.VMEM(msa_block, BF16),
+            pltpu.VMEM(msa_block, BF16),
+            pltpu.VMEM(msa_block, F32),
+            pltpu.VMEM((2, heads * total_res, depth), BF16),
             pltpu.VMEM((2, heads * total_res, depth), BF16),
             pltpu.VMEM((pair_rows, pair_cols, cz), BF16),
             pltpu.VMEM(asking_weights.shape, BF16),
@@ -511,7 +525,7 @@
             pltpu.VMEM(trimult_final_weights.shape, BF16),
             dma((9,)),
         ]
-        + [dma] * 14,
+        + [dma] * 2 + [dma((cols,))] + [dma] * 11,
         compiler_params=pltpu.CompilerParams(
             collective_id=0, has_side_effects=True, vmem_limit_bytes=62 * 2**20
         ),
@@ -537,7 +551,7 @@
         out_shape=tuple(jax.ShapeDtypeStruct(r.shape, r.dtype) for r in results),
         in_specs=[hbm, hbm],
         out_specs=(hbm, hbm),
-        scratch_shapes=[dma((5,))],
+        scratch_shapes=[pltpu.VMEM(r.shape, r.dtype) for r in results] + [dma((5,)), dma((5,))],
         compiler_params=pltpu.CompilerParams(vmem_limit_bytes=62 * 2**20),
     )(*results)
 

time: 53.3 us -> 33.9 us (0.64)
  Pallas kernels: 52.5 us -> 33.1 us
    pallas_call x1, Pallas kernels: 21 us -> 1.91 us  [local_fused(): pl.pallas_call(deliver, out_shape=tuple((jax.ShapeDtypeStruct(r.shape, r....]
where the time goes in v6:
time: 33.9 us; the launch traced here: 33.7 us
  Pallas kernels  33.1 us (98%)
  between operations  0.64 us (2%)
    pallas_call x1, Pallas kernels, local_fused(): pl.pallas_call(functools.partial(fused, (rows, cols, heads, cz)), out_sha...  31.2 us
    pallas_call x1, Pallas kernels, local_fused(): pl.pallas_call(deliver, out_shape=tuple((jax.ShapeDtypeStruct(r.shape, r....  1.91 us

profile of v6, /device:TPU:0, one launch (start us, length us, event | category | flops | bytes accessed | tf_op | source)
XLA Modules:
  0.0 33.7 jit_solution(385743611938445156)
XLA Ops:
  0.6 31.2 %shard_map.149 = (bf16[32,32,256]{2,1,0:T(8,128)(2,1)}, bf16[16,32,128]{2,1,0:T(8,128)(2,1)}) custom-call(bf16[32,32,256]{2,1,0:T(8,128)(2,1)} %x_ref.1, bf16[16,32,128]{2,1,0:T(8,128)(2,1)} %pair_hbm.1, s32[128]{0:T(128)} %flags_smem.1, s32[1,128]{1,0:T(1,128)} %bitcast.4, s32[1,128]{1,0:T(1,128)} %bitcast.5, f32[8]{0:T(128)} %offset_ref.1, ...), custom_call_target="tpu_custom_call" | custom-call | tf_op jit(solution)/shard_map/pallas_call | solution.py:491
  31.8 1.9 %shard_map.150 = (bf16[32,32,256]{2,1,0:T(8,128)(2,1)}, bf16[16,32,128]{2,1,0:T(8,128)(2,1)}) custom-call(bf16[32,32,256]{2,1,0:T(8,128)(2,1)} %get-tuple-element.4.msa_ref, bf16[16,32,128]{2,1,0:T(8,128)(2,1)} %get-tuple-element.5.pair_ref), custom_call_target="tpu_custom_call" | custom-call | tf_op jit(solution)/shard_map/pallas_call | solution.py:549
